TPU v7x, 256 devices: a whole 4x4x8 slice. The times are simulated.
256 devices in a mesh: xy: 64 (over y, x_hi, z), gz: 4 (over x_lo, core).
Axes of the slice: x: 4 (x_hi: 2, x_lo: 2; x = x_hi * 2 + x_lo), y: 4, z: 8, core: 2. Of those that a mesh axis runs over, the one named last changes fastest.
Arguments:
- e_field: float32 [64, 3, 16, 32, 512], P('xy', None, None, None, 'gz'), may hold values from -6 to 6
- h_field: float32 [64, 3, 16, 32, 512], P('xy', None, None, None, 'gz'), may hold values from -6 to 6
- material: int32 [64, 16, 32, 512], P('xy', None, None, 'gz'), may hold values from 0 to 3
- permittivity: float32 [4], replicated, may hold values from 1 to 12
- pml_x: int32 [128], replicated, may hold values from 0 to 8, as said below
- pml_y: int32 [256], replicated, may hold values from 0 to 8, as said below
- pml_z: int32 [512], replicated, may hold values from 0 to 8, as said below
- monitor_z: int32 [3], replicated, may hold values from 8 to 503
- omega: float32 [4], replicated, may hold values from 0.3 to 1.2
- focus: float32 [64, 512], P('xy'), may hold values from 0.1 to 3
Outputs:
- e_out: float32 [64, 3, 16, 32, 512], P('xy', None, None, None, 'gz')
- h_out: float32 [64, 3, 16, 32, 512], P('xy', None, None, None, 'gz')
- spectra: float32 [64, 72, 512], P('xy')
- objective: float32 [], replicated
Inputs may be any that keep to these rules, and one draw needn't show every extreme that they name: `pml_x`: a layer of 4 to 8 cells at each end, level 8 at the outermost cell and 1 or more inside the layer; 0 between the layers. `pml_y`: as pml_x, along the second dimension. `pml_z`: as pml_x, along the third dimension.
All inputs are finite; a program needn't handle non-finite values.
Results may differ from a plain program's by a relative error of at most 0.00007.
Values sent between devices are 32-bit elements; how exact they have to be, the bound alone decides.
A program may use at most 64 MiB of HBM per device.

v0:
```python
import jax
import jax.numpy as jnp
from jax import lax
from jax.sharding import PartitionSpec as P

TILES_Y = 8
STEPS = 4
WAVES = 4
MON = 3
DEPTH = 8


TIME_STEP = 0.5
SIGMA_PEAK = 0.8


def from_behind(value, axis, steps):
    count = lax.axis_size(axis)
    leading, last = (max(0, -steps), min(count, count - steps))
    return lax.ppermute(value, axis, [(source, source + steps) for source in range(leading, last)])


def grade(level):
    scaled = level.astype(jnp.float32) / DEPTH
    return scaled * scaled


def coefficients(permit, sigma):
    loss = sigma * (0.5 * TIME_STEP) / permit
    decay_elec = (1.0 - loss) / (1.0 + loss)
    drive_elec = TIME_STEP / (permit * (1.0 + loss))
    loss_magn = sigma * (0.5 * TIME_STEP)
    decay_magn = (1.0 - loss_magn) / (1.0 + loss_magn)
    drive_magn = TIME_STEP / (1.0 + loss_magn)
    return (decay_elec, drive_elec, decay_magn, drive_magn)


def lower_diff(field, border, axis):
    count = field.shape[axis]
    before = jnp.concatenate(
        [jnp.expand_dims(border, axis), lax.slice_in_dim(field, 0, count - 1, axis=axis)], axis
    )
    return field - before


def upper_diff(field, border, axis):
    count = field.shape[axis]
    after = jnp.concatenate(
        [lax.slice_in_dim(field, 1, count, axis=axis), jnp.expand_dims(border, axis)], axis
    )
    return after - field


def rotate(field, rims, differ):
    first, second, third = rims
    return jnp.stack(
        [
            differ(field[2], second[1], 1) - differ(field[1], third[1], 2),
            differ(field[0], third[0], 2) - differ(field[2], first[1], 0),
            differ(field[1], first[0], 0) - differ(field[0], second[0], 1),
        ]
    )


def lower_rims(hfield, tile_col):
    first = from_behind(hfield[1:3, -1], "xy", TILES_Y)
    second = from_behind(jnp.stack([hfield[0, :, -1], hfield[2, :, -1]]), "xy", 1)
    second = jnp.where(tile_col > 0, second, jnp.zeros_like(second))
    flat = hfield[0:2, :, :, -1]
    third = from_behind(flat.reshape(2, -1), "gz", 1).reshape(flat.shape)
    return (first, second, third)


def upper_rims(efield, tile_col):
    first = from_behind(efield[1:3, 0], "xy", -TILES_Y)
    second = from_behind(jnp.stack([efield[0, :, 0], efield[2, :, 0]]), "xy", -1)
    second = jnp.where(tile_col < TILES_Y - 1, second, jnp.zeros_like(second))
    flat = efield[0:2, :, :, 0]
    third = from_behind(flat.reshape(2, -1), "gz", -1).reshape(flat.shape)
    return (first, second, third)


def curl_with_rims(field, fetch, differ):
    rims = fetch(field)
    return rotate(field, rims, differ)


def body(e_field, h_field, material, permittivity, pml_x, pml_y, pml_z, monitor_z, omega, focus):
    efield = e_field[0]
    hfield = h_field[0]
    rows_first, rows_second, rows_third = (efield.shape[1], efield.shape[2], efield.shape[3])
    tile = lax.axis_index("xy")
    tile_col = tile % TILES_Y
    tile_row = tile // TILES_Y
    slab = lax.axis_index("gz")
    kinds = material[0]
    permit = jnp.zeros(kinds.shape, jnp.float32)
    for which in range(permittivity.shape[0]):
        permit = permit + jnp.where(kinds == which, permittivity[which], 0.0)
    height = slab * rows_third + jnp.arange(rows_third, dtype=jnp.int32)
    select = (height[:, None] == monitor_z[None, :]).astype(jnp.float32)
    plane_cells = rows_first * rows_second
    real_part = jnp.zeros((WAVES, MON * 3, plane_cells), jnp.float32)
    imag_part = jnp.zeros((WAVES, MON * 3, plane_cells), jnp.float32)
    level_first = lax.dynamic_slice_in_dim(pml_x, tile_row * rows_first, rows_first)
    level_second = lax.dynamic_slice_in_dim(pml_y, tile_col * rows_second, rows_second)
    level_third = lax.dynamic_slice_in_dim(pml_z, slab * rows_third, rows_third)
    sigma = SIGMA_PEAK * (
        grade(level_first)[:, None, None]
        + grade(level_second)[None, :, None]
        + grade(level_third)[None, None, :]
    )
    decay_elec, drive_elec, decay_magn, drive_magn = coefficients(permit, sigma)

    def fetch_lower(field):
        return lower_rims(field, tile_col)

    def fetch_upper(field):
        return upper_rims(field, tile_col)

    for instant in range(STEPS):
        curl_magn = curl_with_rims(hfield, fetch_lower, lower_diff)
        efield = decay_elec[None] * efield + drive_elec[None] * curl_magn
        record_real_part = real_part
        record_imag_part = imag_part
        plane = jnp.einsum("cxyz,zm->mcxy", efield, select, precision=lax.Precision.HIGHEST)
        plane = plane.reshape(MON * 3, plane_cells)
        phase = omega * ((instant + 1) * TIME_STEP)
        record_real_part = record_real_part + jnp.cos(phase)[:, None, None] * plane[None]
        record_imag_part = record_imag_part - jnp.sin(phase)[:, None, None] * plane[None]
        real_part = record_real_part
        imag_part = record_imag_part
        curl_elec = curl_with_rims(efield, fetch_upper, upper_diff)
        hfield = decay_magn[None] * hfield - drive_magn[None] * curl_elec
    local_spectra = jnp.concatenate([real_part, imag_part]).reshape(-1, plane_cells)
    half = local_spectra.shape[0] // 2
    count = lax.axis_size("xy") * WAVES * MON * 3 * plane_cells
    weights = focus[0]
    total = lax.psum(local_spectra, "gz")
    partial_term = jnp.sum(weights[None] * (total[:half] ** 2 + total[half:] ** 2))
    objective = lax.psum(partial_term, "xy") / jnp.float32(count)
    return (efield[None], hfield[None], total[None], objective)


def solution(mesh):
    placed = (
        P("xy", None, None, None, "gz"),
        P("xy", None, None, None, "gz"),
        P("xy", None, None, "gz"),
        P(),
        P(),
        P(),
        P(),
        P(),
        P(),
        P("xy", None),
    )
    return jax.shard_map(
        body,
        mesh=mesh,
        in_specs=placed,
        out_specs=(
            P("xy", None, None, None, "gz"),
            P("xy", None, None, None, "gz"),
            P("xy", None, None),
            P(),
        ),
        check_vma=False,
    )
```

profile of v0, /device:TPU:0, one launch (start us, length us, event | category | flops | bytes accessed | tf_op | source)
XLA Modules:
  0.0 451.5 jit_solution(13187191413517148756)
XLA Ops:
  8.8 2.1 collective-permute-start
  11.0 4.9 %collective-permute-start.2 = (f32[2,32,128]{2,1,0:T(8,128)S(1)}, f32[2,32,128]{2,1,0:T(8,128)S(1)}, u32[]{:S(2)}, u32[]{:S(2)}) collective-permute-start(f32[2,32,128]{2,1,0:T(8,128)S(1)} %bitcast.417), channel_id=1, source_target_pairs={{0,32},{4,36},{8,40},{12,44},{16,48},{20,52},{24,56},{28,60},{32,6... | collective-permute-start | bytes 98312 | tf_op jit(solution)/shard_map/ppermute | solution.py:20
  25.9 2.7 divide_bitcast_fusion.1
  42.3 1.8 slice_bitcast_fusion.15
  45.9 2.4 fusion.26
  57.2 4.5 %collective-permute-start.6 = (f32[2,16,128]{2,1,0:T(8,128)S(1)}, f32[2,16,128]{2,1,0:T(8,128)S(1)}, u32[]{:S(2)}, u32[]{:S(2)}) collective-permute-start(f32[2,16,128]{2,1,0:T(8,128)S(1)} %pad_maximum_fusion.3), channel_id=1, source_target_pairs={{0,4},{4,8},{8,12},{12,16},{16,20},{20,24},{24,28},{28,32},{32,36}... | collective-permute-start | bytes 49160 | tf_op jit(solution)/shard_map/ppermute | solution.py:20
  61.7 8.2 %collective-permute-start.8 = (f32[2,32,128]{2,1,0:T(8,128)S(1)}, f32[2,32,128]{2,1,0:T(8,128)}, u32[]{:S(2)}, u32[]{:S(2)}) collective-permute-start(f32[2,32,128]{2,1,0:T(8,128)S(1)} %bitcast.419), channel_id=1, source_target_pairs={{0,32},{4,36},{8,40},{12,44},{16,48},{20,52},{24,56},{28,60},{32,6... | collective-permute-start | bytes 98312 | tf_op jit(solution)/shard_map/ppermute | solution.py:20
  70.3 3.1 collective-permute-start.7
  95.8 5.9 %collective-permute-done.11 = f32[2,32,128]{2,1,0:T(8,128)} collective-permute-done((f32[2,32,128]{2,1,0:T(8,128)}, f32[2,32,128]{2,1,0:T(8,128)}, u32[]{:S(2)}, u32[]{:S(2)}) %collective-permute-start.11) | collective-permute-done | bytes 32800 | tf_op jit(solution)/shard_map/ppermute | solution.py:20
  102.5 2.0 fusion.38
  110.8 8.6 %collective-permute-start.14 = (f32[2,32,128]{2,1,0:T(8,128)S(1)}, f32[2,32,128]{2,1,0:T(8,128)}, u32[]{:S(2)}, u32[]{:S(2)}) collective-permute-start(f32[2,32,128]{2,1,0:T(8,128)S(1)} %bitcast.420), channel_id=1, source_target_pairs={{0,32},{4,36},{8,40},{12,44},{16,48},{20,52},{24,56},{28,60},{32,6... | collective-permute-start | bytes 98312 | tf_op jit(solution)/shard_map/ppermute | solution.py:20
  120.8 4.4 collective-permute-start.13
  130.4 2.0 fusion.41
  146.9 1.9 slice_bitcast_fusion.7
  153.8 2.4 collective-permute-done.17
  157.0 2.0 fusion.44
  164.7 2.1 collective-permute-start.18
  166.8 10.3 %collective-permute-start.20 = (f32[2,32,128]{2,1,0:T(8,128)}, f32[2,32,128]{2,1,0:T(8,128)}, u32[]{:S(2)}, u32[]{:S(2)}) collective-permute-start(f32[2,32,128]{2,1,0:T(8,128)} %bitcast.130), channel_id=1, source_target_pairs={{0,32},{4,36},{8,40},{12,44},{16,48},{20,52},{24,56},{28,60},{32,6... | collective-permute-start | bytes 98312 | tf_op jit(solution)/shard_map/ppermute | solution.py:20
  178.5 3.8 collective-permute-start.19
  184.1 2.9 fusion.18
  210.9 4.9 %collective-permute-done.23 = f32[2,32,128]{2,1,0:T(8,128)S(1)} collective-permute-done((f32[2,32,128]{2,1,0:T(8,128)}, f32[2,32,128]{2,1,0:T(8,128)S(1)}, u32[]{:S(2)}, u32[]{:S(2)}) %collective-permute-start.23) | collective-permute-done | bytes 32800 | tf_op jit(solution)/shard_map/ppermute | solution.py:20
  217.4 36.3 %all-reduce.2.cloned.1.call-done = f32[72,512]{1,0:T(8,128)} async-done(((f32[72,512]{1,0:T(8,128)}), f32[72,512]{1,0:T(8,128)}) %all-reduce.2.cloned.1.call-update) | async-done | bytes 147472 | tf_op jit(solution)/shard_map/psum | solution.py:139
  255.4 2.2 fusion.19
  257.5 184.6 %psum.15 = f32[]{:T(128)} all-reduce(f32[]{:T(128)} %fusion.61), channel_id=1, replica_groups=mesh['xy'=64,'gz'=4] {'xy'}, use_global_device_ids=true, to_apply=%region_2.3 | all-reduce | flops 1 | bytes 8 | tf_op jit(solution)/shard_map/psum | solution.py:141
  (442 shorter events, 128.1 us)
Async XLA Ops:
  7.2 246.6 %all-reduce.2.cloned.1.call-start = ((), (), s32[]{:S(2)}) async-start(), calls=%async_computation | async-start | bytes 294912 | tf_op jit(solution)/shard_map/psum | solution.py:139
  8.8 23.5 %collective-permute-start = (f32[2,16,128]{2,1,0:T(8,128)S(1)}, f32[2,16,128]{2,1,0:T(8,128)S(1)}, u32[]{:S(2)}, u32[]{:S(2)}) collective-permute-start(f32[2,16,128]{2,1,0:T(8,128)S(1)} %pad_maximum_fusion.1), channel_id=1, source_target_pairs={{0,4},{4,8},{8,12},{12,16},{16,20},{20,24},{24,28},{28,32},{32,36}... | collective-permute-start | bytes 49160 | tf_op jit(solution)/shard_map/ppermute | solution.py:20
  11.0 21.4 %collective-permute-start.2 = (f32[2,32,128]{2,1,0:T(8,128)S(1)}, f32[2,32,128]{2,1,0:T(8,128)S(1)}, u32[]{:S(2)}, u32[]{:S(2)}) collective-permute-start(f32[2,32,128]{2,1,0:T(8,128)S(1)} %bitcast.417), channel_id=1, source_target_pairs={{0,32},{4,36},{8,40},{12,44},{16,48},{20,52},{24,56},{28,60},{32,6... | collective-permute-start | bytes 98312 | tf_op jit(solution)/shard_map/ppermute | solution.py:20
  16.5 13.3 %collective-permute-start.1 = (f32[2,512]{1,0:T(2,128)S(1)}, f32[2,512]{1,0:T(2,128)S(1)}, u32[]{:S(2)}, u32[]{:S(2)}) collective-permute-start(f32[2,512]{1,0:T(2,128)S(1)} %reshape_squeeze.24), channel_id=1, source_target_pairs={{0,1},{1,2},{2,3},{4,5},{5,6},{6,7},{8,9},{9,10},{10,11},{12,13},{... | collective-permute-start | bytes 12296 | tf_op jit(solution)/shard_map/ppermute | solution.py:20
  37.4 13.0 %collective-permute-start.3 = (f32[2,16,128]{2,1,0:T(8,128)S(1)}, f32[2,16,128]{2,1,0:T(8,128)}, u32[]{:S(2)}, u32[]{:S(2)}) collective-permute-start(f32[2,16,128]{2,1,0:T(8,128)S(1)} %pad_maximum_fusion.2), channel_id=1, source_target_pairs={{4,0},{8,4},{12,8},{16,12},{20,16},{24,20},{28,24},{32,28},{36,32}... | collective-permute-start | bytes 49160 | tf_op jit(solution)/shard_map/ppermute | solution.py:20
  38.7 12.4 %collective-permute-start.5 = (f32[2,32,128]{2,1,0:T(8,128)S(1)}, f32[2,32,128]{2,1,0:T(8,128)}, u32[]{:S(2)}, u32[]{:S(2)}) collective-permute-start(f32[2,32,128]{2,1,0:T(8,128)S(1)} %bitcast.418), channel_id=1, source_target_pairs={{32,0},{36,4},{40,8},{44,12},{48,16},{52,20},{56,24},{60,28},{64,3... | collective-permute-start | bytes 98312 | tf_op jit(solution)/shard_map/ppermute | solution.py:20
  41.0 8.1 %collective-permute-start.4 = (f32[2,512]{1,0:T(2,128)}, f32[2,512]{1,0:T(2,128)S(1)}, u32[]{:S(2)}, u32[]{:S(2)}) collective-permute-start(f32[2,512]{1,0:T(2,128)} %reshape_squeeze.25), channel_id=1, source_target_pairs={{1,0},{2,1},{3,2},{5,4},{6,5},{7,6},{9,8},{10,9},{11,10},{13,12},{... | collective-permute-start | bytes 12296 | tf_op jit(solution)/shard_map/ppermute | solution.py:20
  57.2 19.3 %collective-permute-start.6 = (f32[2,16,128]{2,1,0:T(8,128)S(1)}, f32[2,16,128]{2,1,0:T(8,128)S(1)}, u32[]{:S(2)}, u32[]{:S(2)}) collective-permute-start(f32[2,16,128]{2,1,0:T(8,128)S(1)} %pad_maximum_fusion.3), channel_id=1, source_target_pairs={{0,4},{4,8},{8,12},{12,16},{16,20},{20,24},{24,28},{28,32},{32,36}... | collective-permute-start | bytes 49160 | tf_op jit(solution)/shard_map/ppermute | solution.py:20
  61.7 14.8 %collective-permute-start.8 = (f32[2,32,128]{2,1,0:T(8,128)S(1)}, f32[2,32,128]{2,1,0:T(8,128)}, u32[]{:S(2)}, u32[]{:S(2)}) collective-permute-start(f32[2,32,128]{2,1,0:T(8,128)S(1)} %bitcast.419), channel_id=1, source_target_pairs={{0,32},{4,36},{8,40},{12,44},{16,48},{20,52},{24,56},{28,60},{32,6... | collective-permute-start | bytes 98312 | tf_op jit(solution)/shard_map/ppermute | solution.py:20
  70.3 4.9 %collective-permute-start.7 = (f32[2,512]{1,0:T(2,128)S(1)}, f32[2,512]{1,0:T(2,128)S(1)}, u32[]{:S(2)}, u32[]{:S(2)}) collective-permute-start(f32[2,512]{1,0:T(2,128)S(1)} %reshape_squeeze.26), channel_id=1, source_target_pairs={{0,1},{1,2},{2,3},{4,5},{5,6},{6,7},{8,9},{9,10},{10,11},{12,13},{... | collective-permute-start | bytes 12296 | tf_op jit(solution)/shard_map/ppermute | solution.py:20
  86.0 9.0 %collective-permute-start.9 = (f32[2,16,128]{2,1,0:T(8,128)}, f32[2,16,128]{2,1,0:T(8,128)}, u32[]{:S(2)}, u32[]{:S(2)}) collective-permute-start(f32[2,16,128]{2,1,0:T(8,128)} %pad_maximum_fusion.4), channel_id=1, source_target_pairs={{4,0},{8,4},{12,8},{16,12},{20,16},{24,20},{28,24},{32,28},{36,32}... | collective-permute-start | bytes 49160 | tf_op jit(solution)/shard_map/ppermute | solution.py:20
  87.3 14.3 %collective-permute-start.11 = (f32[2,32,128]{2,1,0:T(8,128)}, f32[2,32,128]{2,1,0:T(8,128)}, u32[]{:S(2)}, u32[]{:S(2)}) collective-permute-start(f32[2,32,128]{2,1,0:T(8,128)} %bitcast.81), channel_id=1, source_target_pairs={{32,0},{36,4},{40,8},{44,12},{48,16},{52,20},{56,24},{60,28},{64,3... | collective-permute-start | bytes 98312 | tf_op jit(solution)/shard_map/ppermute | solution.py:20
  109.5 20.1 %collective-permute-start.12 = (f32[2,16,128]{2,1,0:T(8,128)S(1)}, f32[2,16,128]{2,1,0:T(8,128)S(1)}, u32[]{:S(2)}, u32[]{:S(2)}) collective-permute-start(f32[2,16,128]{2,1,0:T(8,128)S(1)} %pad_maximum_fusion.5), channel_id=1, source_target_pairs={{0,4},{4,8},{8,12},{12,16},{16,20},{20,24},{24,28},{28,32},{32,36}... | collective-permute-start | bytes 49160 | tf_op jit(solution)/shard_map/ppermute | solution.py:20
  110.8 18.8 %collective-permute-start.14 = (f32[2,32,128]{2,1,0:T(8,128)S(1)}, f32[2,32,128]{2,1,0:T(8,128)}, u32[]{:S(2)}, u32[]{:S(2)}) collective-permute-start(f32[2,32,128]{2,1,0:T(8,128)S(1)} %bitcast.420), channel_id=1, source_target_pairs={{0,32},{4,36},{8,40},{12,44},{16,48},{20,52},{24,56},{28,60},{32,6... | collective-permute-start | bytes 98312 | tf_op jit(solution)/shard_map/ppermute | solution.py:20
  120.8 6.8 %collective-permute-start.13 = (f32[2,512]{1,0:T(2,128)S(1)}, f32[2,512]{1,0:T(2,128)S(1)}, u32[]{:S(2)}, u32[]{:S(2)}) collective-permute-start(f32[2,512]{1,0:T(2,128)S(1)} %reshape_squeeze.28), channel_id=1, source_target_pairs={{0,1},{1,2},{2,3},{4,5},{5,6},{6,7},{8,9},{9,10},{10,11},{12,13},{... | collective-permute-start | bytes 12296 | tf_op jit(solution)/shard_map/ppermute | solution.py:20
  141.0 12.0 %collective-permute-start.15 = (f32[2,16,128]{2,1,0:T(8,128)}, f32[2,16,128]{2,1,0:T(8,128)}, u32[]{:S(2)}, u32[]{:S(2)}) collective-permute-start(f32[2,16,128]{2,1,0:T(8,128)} %pad_maximum_fusion.6), channel_id=1, source_target_pairs={{4,0},{8,4},{12,8},{16,12},{20,16},{24,20},{28,24},{32,28},{36,32}... | collective-permute-start | bytes 49160 | tf_op jit(solution)/shard_map/ppermute | solution.py:20
  142.3 13.9 %collective-permute-start.17 = (f32[2,32,128]{2,1,0:T(8,128)}, f32[2,32,128]{2,1,0:T(8,128)}, u32[]{:S(2)}, u32[]{:S(2)}) collective-permute-start(f32[2,32,128]{2,1,0:T(8,128)} %bitcast.114), channel_id=1, source_target_pairs={{32,0},{36,4},{40,8},{44,12},{48,16},{52,20},{56,24},{60,28},{64,3... | collective-permute-start | bytes 98312 | tf_op jit(solution)/shard_map/ppermute | solution.py:20
  145.6 5.5 %collective-permute-start.16 = (f32[2,512]{1,0:T(2,128)}, f32[2,512]{1,0:T(2,128)S(1)}, u32[]{:S(2)}, u32[]{:S(2)}) collective-permute-start(f32[2,512]{1,0:T(2,128)} %reshape_squeeze.29), channel_id=1, source_target_pairs={{1,0},{2,1},{3,2},{5,4},{6,5},{7,6},{9,8},{10,9},{11,10},{13,12},{... | collective-permute-start | bytes 12296 | tf_op jit(solution)/shard_map/ppermute | solution.py:20
  164.7 24.3 %collective-permute-start.18 = (f32[2,16,128]{2,1,0:T(8,128)S(1)}, f32[2,16,128]{2,1,0:T(8,128)S(1)}, u32[]{:S(2)}, u32[]{:S(2)}) collective-permute-start(f32[2,16,128]{2,1,0:T(8,128)S(1)} %pad_maximum_fusion.7), channel_id=1, source_target_pairs={{0,4},{4,8},{8,12},{12,16},{16,20},{20,24},{24,28},{28,32},{32,36}... | collective-permute-start | bytes 49160 | tf_op jit(solution)/shard_map/ppermute | solution.py:20
  166.8 22.2 %collective-permute-start.20 = (f32[2,32,128]{2,1,0:T(8,128)}, f32[2,32,128]{2,1,0:T(8,128)}, u32[]{:S(2)}, u32[]{:S(2)}) collective-permute-start(f32[2,32,128]{2,1,0:T(8,128)} %bitcast.130), channel_id=1, source_target_pairs={{0,32},{4,36},{8,40},{12,44},{16,48},{20,52},{24,56},{28,60},{32,6... | collective-permute-start | bytes 98312 | tf_op jit(solution)/shard_map/ppermute | solution.py:20
  178.5 9.2 %collective-permute-start.19 = (f32[2,512]{1,0:T(2,128)S(1)}, f32[2,512]{1,0:T(2,128)S(1)}, u32[]{:S(2)}, u32[]{:S(2)}) collective-permute-start(f32[2,512]{1,0:T(2,128)S(1)} %reshape_squeeze.30), channel_id=1, source_target_pairs={{0,1},{1,2},{2,3},{4,5},{5,6},{6,7},{8,9},{9,10},{10,11},{12,13},{... | collective-permute-start | bytes 12296 | tf_op jit(solution)/shard_map/ppermute | solution.py:20
  200.4 10.5 %collective-permute-start.21 = (f32[2,16,128]{2,1,0:T(8,128)S(1)}, f32[2,16,128]{2,1,0:T(8,128)S(1)}, u32[]{:S(2)}, u32[]{:S(2)}) collective-permute-start(f32[2,16,128]{2,1,0:T(8,128)S(1)} %pad_maximum_fusion.8), channel_id=1, source_target_pairs={{4,0},{8,4},{12,8},{16,12},{20,16},{24,20},{28,24},{32,28},{36,32}... | collective-permute-start | bytes 49160 | tf_op jit(solution)/shard_map/ppermute | solution.py:20
  201.7 14.1 %collective-permute-start.23 = (f32[2,32,128]{2,1,0:T(8,128)}, f32[2,32,128]{2,1,0:T(8,128)S(1)}, u32[]{:S(2)}, u32[]{:S(2)}) collective-permute-start(f32[2,32,128]{2,1,0:T(8,128)} %slice_bitcast_fusion.61), channel_id=1, source_target_pairs={{32,0},{36,4},{40,8},{44,12},{48,16},{52,20},{56,24},{60,28},{64,3... | collective-permute-start | bytes 98312 | tf_op jit(solution)/shard_map/ppermute | solution.py:20
  205.1 4.0 collective-permute-start.22
  (102 other events, 451.7 us)
Sparse Core Ops, SparseCore 0:
  204.9 48.8 all-reduce.1
where the time goes:
time: 454 us; the launch traced here: 451 us
  blocking collectives  185 us (41%)
  local copies, waits for them, and re-layouts  83.6 us (18%)
  starting transfers between devices  70.5 us (16%)
  waiting for transfers between devices  51.4 us (11%)
  other arithmetic  37.5 us (8%)
  between operations  17.4 us (4%)
  matrix products  6.55 us (1%)
    psum x1, blocking collectives, body(): objective = lax.psum(partial_term, 'xy') / jnp.float32(count)  185 us
    ppermute x24, starting transfers between devices, from_behind(): lax.ppermute(value, axis, [(source, source + steps) for source in range(l...  70.4 us
    psum x1, waiting for transfers between devices, body(): total = lax.psum(local_spectra, 'gz')  36.3 us
    concatenate x39, local copies, waits for them, and re-layouts, lower_diff(): jnp.concatenate([jnp.expand_dims(border, axis), lax.slice_in_dim(field, 0...  20.1 us
    concatenate x34, local copies, waits for them, and re-layouts, upper_diff(): jnp.concatenate([lax.slice_in_dim(field, 1, count, axis=axis), jnp.expand...  18.6 us
    ppermute x24, waiting for transfers between devices, from_behind(): lax.ppermute(value, axis, [(source, source + steps) for source in range(l...  15.1 us
    sub x8, other arithmetic, rotate(): differ(field[2], second[1], 1) - differ(field[1], third[1], 2)  14.7 us
    unnamed x206, local copies, waits for them, and re-layouts  10.8 us
  transfers between devices with their start and end apart: 25, of which 6 were waited for; matrix products, arithmetic and copies ran while one was open for 13% of the time, Pallas kernels for 0%

commit v1 on v0

v1 whole, which is shorter than its diff:
```python
import functools

import jax
import jax.numpy as jnp
from jax import lax
from jax.experimental import pallas as pl
from jax.experimental.pallas import tpu as pltpu
from jax.sharding import PartitionSpec as P

MESH = pl.DeviceIdType.MESH
TILES_X = 8
TILES_Y = 8
SLABS = 4
STEPS = 4
WAVES = 4
MON = 3
DEPTH = 8
TIME_STEP = 0.5
SIGMA_PEAK = 0.8
CX, CY, CZ = 16, 32, 128
F32 = jnp.float32
EDGES = ((1, 0, -1), (-1, 0, 1), (1, -1, 0), (-1, 1, 0), (0, 1, -1), (0, -1, 1))


def roll(value, shift, axis):
    return pltpu.roll(value, shift % value.shape[axis], axis)


def grade(level):
    scaled = level.astype(F32) / DEPTH
    return scaled * scaled


def magnetic(sigma):
    loss = sigma * (0.5 * TIME_STEP)
    return (1.0 - loss) / (1.0 + loss), TIME_STEP / (1.0 + loss)


def electric(sigma, permit):
    loss = sigma * (0.5 * TIME_STEP) / permit
    return (1.0 - loss) / (1.0 + loss), TIME_STEP / (permit * (1.0 + loss))


def kernel(
    e_in, h_in, m_in, focus, permit, pml_x, pml_y, pml_z, monitor, omega,
    e_out, h_out, spec, objective,
    es, hs, kinds, ca, cb, da, db, grades_x, grades_y, trig, acc, planes, first, second,
    hy, hz, dax, day, daz,
    s_hy, s_hz, r_hx, r_hy, r_hz,
    s_ey, s_ez, r_ex, r_ey, r_ez,
    s_uy, s_uz, r_ux, r_uy, r_uz, r_edge,
    local_sem, send_sem, recv_sem, plane_send, plane_recv, total_send, total_recv,
):
    tile = lax.axis_index("xy")
    slab = lax.axis_index("gz")
    row, col = tile // TILES_Y, tile % TILES_Y

    def valid(off):
        r, c, g = row + off[0], col + off[1], slab + off[2]
        return (r >= 0) & (r < TILES_X) & (c >= 0) & (c < TILES_Y) & (g >= 0) & (g < SLABS)

    def device(off):
        return ((row + off[0]) * TILES_Y + col + off[1], slab + off[2])

    def minus(off):
        return tuple(-o for o in off)

    class Move:
        def __init__(self, n, k, off, src, dst):
            self.off = off
            self.copy = lambda: pltpu.make_async_remote_copy(
                src_ref=src, dst_ref=dst, send_sem=send_sem.at[n, k], recv_sem=recv_sem.at[n, k],
                device_id=device(off), device_id_type=MESH)

        def start(self):
            @pl.when(valid(self.off))
            def _():
                self.copy().start()

        def wait_send(self):
            @pl.when(valid(self.off))
            def _():
                self.copy().wait_send()

        def wait_recv(self):
            @pl.when(valid(minus(self.off)))
            def _():
                self.copy().wait_recv()

    barrier = pltpu.get_barrier_semaphore()

    def greet(where):
        pl.semaphore_signal(barrier, inc=1, device_id=where, device_id_type=MESH)

    for i in range(1, TILES_Y):
        greet((row * TILES_Y + (col + i) % TILES_Y, slab))
    for i in range(1, TILES_X):
        greet(((row + i) % TILES_X * TILES_Y + col, slab))
    for i in range(1, SLABS):
        greet((tile, (slab + i) % SLABS))
    for off in EDGES:
        @pl.when(valid(off))
        def _(off=off):
            greet(device(off))

    loads = []
    for k in range(3):
        loads.append(pltpu.make_async_copy(
            h_in.at[0, k], hs.at[k, pl.ds(1, CX), pl.ds(8, CY), :], local_sem.at[k]))
    loads.append(pltpu.make_async_copy(m_in.at[0], kinds, local_sem.at[3]))
    for k in range(3):
        loads.append(pltpu.make_async_copy(
            e_in.at[0, k], es.at[k, pl.ds(0, CX), pl.ds(0, CY), :], local_sem.at[4 + k]))
    for load in loads:
        load.start()

    lane8 = lax.broadcasted_iota(jnp.int32, (8, 128), 1)
    row8 = lax.broadcasted_iota(jnp.int32, (8, 128), 0)
    lane16 = lax.broadcasted_iota(jnp.int32, (16, 128), 1)
    row16 = lax.broadcasted_iota(jnp.int32, (16, 128), 0)
    lane32 = lax.broadcasted_iota(jnp.int32, (CY, 128), 1)
    row32 = lax.broadcasted_iota(jnp.int32, (CY, 128), 0)
    zero8 = jnp.zeros((8, 128), F32)

    def clear(off, *refs):
        @pl.when(jnp.logical_not(valid(minus(off))))
        def _():
            for ref in refs:
                ref[...] = jnp.zeros(ref.shape, F32)

    clear((1, 0, 0), r_hx, r_ux)
    clear((0, 1, 0), r_hy, r_uy)
    clear((0, 0, 1), r_hz, r_uz)
    clear((-1, 0, 0), r_ex)
    clear((0, -1, 0), r_ey)
    clear((0, 0, -1), r_ez)
    for k, off in enumerate(EDGES):
        clear(off, r_edge.at[k])

    def pack(total, field, source, start):
        for k in range(CY // 8):
            piece = roll(field[8 * k:8 * k + 8], start + k - source, 1)
            total = jnp.where(lane8 == start + k, piece, total)
        return total

    def unpack(packed, start, target):
        return jnp.concatenate([roll(packed, target - start - k, 1) for k in range(CY // 8)], axis=0)

    for k in range(3):
        loads[k].wait()

    def pack_h(x, total):
        total = roll(total, -4, 1)
        h0 = hs[0, x + 1, 8:8 + CY, :]
        h1 = hs[1, x + 1, 8:8 + CY, :]
        s_hy[0, pl.ds(x, 1), :] = h0[CY - 1:CY]
        s_hy[1, pl.ds(x, 1), :] = hs[2, x + 1, 7 + CY:8 + CY, :]
        return pack(pack(total, h0, 127, 60), h1, 127, 124)

    s_hz[...] = lax.fori_loop(0, CX, pack_h, zero8)

    greeted = TILES_Y - 1 + TILES_X - 1 + SLABS - 1
    for off in EDGES:
        greeted = greeted + jnp.where(valid(off), 1, 0)
    pl.semaphore_wait(barrier, greeted)

    opening = [
        Move(STEPS, 0, (1, 0, 0), hs.at[pl.ds(1, 2), CX, pl.ds(8, CY), :], r_hx),
        Move(STEPS, 1, (0, 1, 0), s_hy, r_hy),
        Move(STEPS, 2, (0, 0, 1), s_hz, r_hz),
    ]
    for move in opening:
        move.start()

    for i in range(CX):
        grades_x[i:i + 1, :] = jnp.full((1, 128), grade(pml_x[row * CX + i]), F32)
    for j in range(CY):
        grades_y[j:j + 1, :] = jnp.full((1, 128), grade(pml_y[col * CY + j]), F32)

    def lay(k, levels):
        return jnp.where(lane8 == k, pml_z[slab * CZ + k], levels)

    along_z = grade(lax.fori_loop(0, CZ, lay, jnp.zeros((8, 128), jnp.int32)))
    along_z32 = jnp.concatenate([along_z] * 4, axis=0)

    loads[3].wait()

    def fill(x, _):
        g = jnp.full((CY, 128), grade(pml_x[row * CX + x]), F32)
        sigma = SIGMA_PEAK * ((g + grades_y[...]) + along_z32)
        kind = kinds[x]
        eps = jnp.full((CY, 128), permit[0], F32)
        for which in range(1, 4):
            eps = jnp.where(kind == which, permit[which], eps)
        ca[x], cb[x] = electric(sigma, eps)
        da[x], db[x] = magnetic(sigma)
        return 0

    lax.fori_loop(0, CX, fill, 0)

    def below(ref, off, sigma):
        inside = jnp.where(valid(off), 1.0, 0.0).astype(F32)
        decay, drive = magnetic(sigma)
        ref[0] = decay * inside
        ref[1] = drive * inside

    g = grade(pml_x[jnp.maximum(row * CX - 1, 0)])
    below(dax, (-1, 0, 0), SIGMA_PEAK * ((g + grades_y[...]) + along_z32))
    g = grade(pml_y[jnp.maximum(col * CY - 1, 0)])
    below(day, (0, -1, 0), SIGMA_PEAK * ((grades_x[...] + g) + along_z32[0:CX]))
    g = grade(pml_z[jnp.maximum(slab * CZ - 1, 0)])
    packed_x = zero8
    for i in range(CX):
        packed_x = jnp.where((lane8 % 64) // 4 == i, grades_x[i:i + 1, :], packed_x)
    packed_y = zero8
    for k in range(CY // 8):
        packed_y = jnp.where(lane8 % 4 == k, grades_y[8 * k:8 * k + 8, :], packed_y)
    below(daz, (0, 0, -1), SIGMA_PEAK * ((packed_x + packed_y) + g))

    for n in range(STEPS):
        for w in range(WAVES):
            phase = jnp.full((8, 128), omega[w] * ((n + 1) * TIME_STEP), F32)
            trig[0, w, n] = jnp.cos(phase)
            trig[1, w, n] = -jnp.sin(phase)
    acc[...] = jnp.zeros(acc.shape, F32)

    for k in range(3):
        loads[4 + k].wait()
    for move in opening:
        move.wait_recv()
    hs[1, 0, 8:8 + CY, :] = r_hx[0]
    hs[2, 0, 8:8 + CY, :] = r_hx[1]
    hy[...] = r_hy[...]
    hz[...] = r_hz[...]
    for move in opening:
        move.wait_send()

    def electric_phase(n):
        def body(x, carry):
            halo, low, high, high2 = carry
            hs[0, x + 1, 7:8, :] = hy[0, pl.ds(x, 1), :]
            hs[2, x + 1, 7:8, :] = hy[1, pl.ds(x, 1), :]
            h0 = hs[0, x + 1, 8:8 + CY, :]
            h1 = hs[1, x + 1, 8:8 + CY, :]
            h2 = hs[2, x + 1, 8:8 + CY, :]
            h0y = hs[0, x + 1, 7:7 + CY, :]
            h2y = hs[2, x + 1, 7:7 + CY, :]
            h1x = hs[1, x, 8:8 + CY, :]
            h2x = hs[2, x, 8:8 + CY, :]
            h0z = jnp.where(lane32 == 0, unpack(halo, 0, 0), roll(h0, 1, 1))
            h1z = jnp.where(lane32 == 0, unpack(halo, 64, 0), roll(h1, 1, 1))
            decay, drive = ca[x], cb[x]
            e0 = decay * es[0, x, 0:CY, :] + drive * ((h2 - h2y) - (h1 - h1z))
            e1 = decay * es[1, x, 0:CY, :] + drive * ((h0 - h0z) - (h2 - h2x))
            e2 = decay * es[2, x, 0:CY, :] + drive * ((h1 - h1x) - (h0 - h0y))
            es[0, x, 0:CY, :] = e0
            es[1, x, 0:CY, :] = e1
            es[2, x, 0:CY, :] = e2
            s_ey[n, 0, pl.ds(x, 1), :] = e0[0:1]
            s_ey[n, 1, pl.ds(x, 1), :] = e2[0:1]
            low = pack(pack(roll(low, -4, 1), e0, 0, 60), e1, 0, 124)
            if n < STEPS - 1:
                for k, e in enumerate((e0, e1, e2)):
                    s_uy[n, k, pl.ds(x, 1), :] = e[CY - 1:CY]
                high = pack(pack(roll(high, -4, 1), e0, 127, 60), e1, 127, 124)
                high2 = pack(pack(roll(high2, -4, 1), e2, 127, 60), e2, 127, 124)
            return roll(halo, -4, 1), low, high, high2

        _, low, high, high2 = lax.fori_loop(0, CX, body, (hz[...], zero8, zero8, zero8))
        s_ez[n] = low
        if n < STEPS - 1:
            s_uz[n, 0] = high
            s_uz[n, 1] = high2

    def electric_moves(n):
        moves = [
            Move(n, 0, (-1, 0, 0), es.at[pl.ds(1, 2), 0, pl.ds(0, CY), :], r_ex.at[n]),
            Move(n, 1, (0, -1, 0), s_ey.at[n], r_ey.at[n]),
            Move(n, 2, (0, 0, -1), s_ez.at[n], r_ez.at[n]),
        ]
        if n == STEPS - 1:
            return moves
        sources = (s_ez.at[n], s_uz.at[n, 1], es.at[0, CX - 1, pl.ds(0, 8), :], es.at[1, 0, pl.ds(CY - 8, 8), :], s_ez.at[n], s_uz.at[n, 1])
        edges = [Move(n, 6 + k, off, sources[k], r_edge.at[k, n]) for k, off in enumerate(EDGES)]
        return [
            edges[2], edges[3],
            Move(n, 3, (1, 0, 0), es.at[:, CX - 1, pl.ds(0, CY), :], r_ux.at[n]),
            moves[0],
            Move(n, 4, (0, 1, 0), s_uy.at[n], r_uy.at[n]),
            moves[1], edges[0], edges[1], edges[4], edges[5],
            Move(n, 5, (0, 0, 1), s_uz.at[n], r_uz.at[n]),
            moves[2],
        ]

    def below_phase(n):
        e0, e1, e2 = r_ux[n, 0], r_ux[n, 1], r_ux[n, 2]
        e0z = jnp.where(lane32 == 127, unpack(r_edge[0, n], 60, 127), roll(e0, -1, 1))
        e0y = jnp.where(row32 == CY - 1, r_edge[2, n, 0:1, :], roll(e0, -1, 0))
        h1 = hs[1, 0, 8:8 + CY, :]
        h2 = hs[2, 0, 8:8 + CY, :]
        hs[1, 0, 8:8 + CY, :] = dax[0] * h1 - dax[1] * ((e0z - e0) - (es[2, 0, 0:CY, :] - e2))
        hs[2, 0, 8:8 + CY, :] = dax[0] * h2 - dax[1] * ((es[1, 0, 0:CY, :] - e1) - (e0y - e0))

        e0, e1, e2 = r_uy[n, 0], r_uy[n, 1], r_uy[n, 2]
        corner = jnp.broadcast_to(r_edge[4, n, 7:8, :], (CX, 128))
        corner = jnp.sum(jnp.where(lane16 == 67 + 4 * row16, corner, 0.0), axis=1, keepdims=True)
        e1z = jnp.where(lane16 == 127, corner, roll(e1, -1, 1))
        e1x = jnp.where(row16 == CX - 1, r_edge[3, n, 7:8, :], roll(e1, -1, 0))
        hy[0] = day[0] * hy[0] - day[1] * ((s_ey[n, 1] - e2) - (e1z - e1))
        hy[1] = day[0] * hy[1] - day[1] * ((e1x - e1) - (s_ey[n, 0] - e0))

        e2 = r_uz[n, 1]
        along = roll(s_ez[n] - r_uz[n, 0], 64, 1)
        up = roll(e2, -1, 0)
        up_next = roll(up, -1, 1)
        up_edge = roll(roll(r_edge[5, n], -1, 0), 3, 1)
        e2y = jnp.where(row8 < 7, up, jnp.where(lane8 % 4 == 3, up_edge, up_next))
        e2x = jnp.where(lane8 >= 124, roll(r_edge[1, n], 124, 1), roll(e2, -4, 1))
        curl = jnp.where(lane8 < 64, (e2y - e2) - along, along - (e2x - e2))
        hz[...] = daz[0] * hz[...] - daz[1] * curl

    def magnetic_phase(n):
        es[1, CX, 0:CY, :] = r_ex[n, 0]
        es[2, CX, 0:CY, :] = r_ex[n, 1]

        def body(x, halo):
            es[0, x, CY:CY + 1, :] = r_ey[n, 0, pl.ds(x, 1), :]
            es[2, x, CY:CY + 1, :] = r_ey[n, 1, pl.ds(x, 1), :]
            e0 = es[0, x, 0:CY, :]
            e1 = es[1, x, 0:CY, :]
            e2 = es[2, x, 0:CY, :]
            e0y = es[0, x, 1:1 + CY, :]
            e2y = es[2, x, 1:1 + CY, :]
            e1x = es[1, x + 1, 0:CY, :]
            e2x = es[2, x + 1, 0:CY, :]
            e0z = jnp.where(lane32 == 127, unpack(halo, 0, 127), roll(e0, -1, 1))
            e1z = jnp.where(lane32 == 127, unpack(halo, 64, 127), roll(e1, -1, 1))
            decay, drive = da[x], db[x]
            hs[0, x + 1, 8:8 + CY, :] = decay * hs[0, x + 1, 8:8 + CY, :] - drive * ((e2y - e2) - (e1z - e1))
            hs[1, x + 1, 8:8 + CY, :] = decay * hs[1, x + 1, 8:8 + CY, :] - drive * ((e0z - e0) - (e2x - e2))
            hs[2, x + 1, 8:8 + CY, :] = decay * hs[2, x + 1, 8:8 + CY, :] - drive * ((e1x - e1) - (e0y - e0))
            return roll(halo, -4, 1)

        lax.fori_loop(0, CX, body, r_ez[n])

    def extract_planes(n):
        weights = []
        for c in range(3):
            weight = jnp.zeros((16, 128), F32)
            for p in range(MON):
                weight = jnp.where((row16 == 3 * p + c) & (lane16 + slab * CZ == monitor[p]), 1.0, weight)
            weights.append(weight.astype(jnp.bfloat16))
        planes[n, slab, 32:40, :] = zero8

        for k in range(CX // 4):
            total = jnp.zeros((16, 128), F32)
            for c in range(3):
                rest = es[c, 4 * k:4 * k + 4, 0:CY, :].reshape(128, 128)
                for _ in range(3):
                    piece = rest.astype(jnp.bfloat16)
                    rest = rest - piece.astype(F32)
                    total = total + lax.dot_general(
                        weights[c], piece, (((1,), (1,)), ((), ())), preferred_element_type=F32)
            planes[n, slab, 8 * k:8 * k + 8, :] = total[0:8]
            planes[n, slab, 32 + k:33 + k, :] = total[8:9]

    def plane_move(n, i):
        return pltpu.make_async_remote_copy(
            src_ref=planes.at[n, slab], dst_ref=planes.at[n, slab],
            send_sem=plane_send.at[n, i - 1], recv_sem=plane_recv.at[n, i - 1],
            device_id=(tile, (slab + i) % SLABS), device_id_type=MESH)

    def plane_arrival(n, i):
        source = (slab + SLABS - i) % SLABS
        return pltpu.make_async_remote_copy(
            src_ref=planes.at[n, source], dst_ref=planes.at[n, source],
            send_sem=plane_send.at[n, i - 1], recv_sem=plane_recv.at[n, i - 1],
            device_id=(tile, (slab + i) % SLABS), device_id_type=MESH)

    def accumulate(n):
        for i in range(1, SLABS):
            plane_arrival(n, i).wait_recv()
        for k in range(5):
            whole = planes[n, 0, 8 * k:8 * k + 8, :]
            for g in range(1, SLABS):
                whole = whole + planes[n, g, 8 * k:8 * k + 8, :]
            for q in range(2):
                for w in range(WAVES):
                    acc[q, w, k] = acc[q, w, k] + trig[q, w, n] * whole

    for n in range(STEPS):
        electric_phase(n)
        moves = electric_moves(n)
        for move in moves:
            move.start()
        extract_planes(n)
        for i in range(1, SLABS):
            plane_move(n, i).start()
        if n == STEPS - 1:
            break
        if n:
            accumulate(n - 1)
        for move in moves:
            move.wait_recv()
        magnetic_phase(n)
        below_phase(n)
        for move in moves:
            move.wait_send()

    stores = [pltpu.make_async_copy(
        es.at[k, pl.ds(0, CX), pl.ds(0, CY), :], e_out.at[0, k], local_sem.at[7 + k]) for k in range(3)]
    for store in stores:
        store.start()
    accumulate(STEPS - 2)
    accumulate(STEPS - 1)

    part = jnp.zeros((1, 128), F32)
    odd = jnp.zeros((8, 128), F32)
    for w in range(WAVES):
        odd = odd + (acc[0, w, 4] * acc[0, w, 4] + acc[1, w, 4] * acc[1, w, 4])
    for k in range(4):
        power = jnp.zeros((8, 128), F32)
        for w in range(WAVES):
            power = power + (acc[0, w, k] * acc[0, w, k] + acc[1, w, k] * acc[1, w, k])
        power = jnp.sum(power, axis=0, keepdims=True) + odd[k:k + 1]
        part = part + power * focus[0:1, 128 * k:128 * k + 128]

    def total_moves(stage, count, mine, where):
        buf = (first, second)[stage]

        def one(slot, i):
            return pltpu.make_async_remote_copy(
                src_ref=buf.at[pl.ds(slot, 1), :], dst_ref=buf.at[pl.ds(slot, 1), :],
                send_sem=total_send.at[stage, i], recv_sem=total_recv.at[stage, i],
                device_id=where(i), device_id_type=MESH)

        return ([one(mine, i) for i in range(1, count)],
                [one((mine + count - i) % count, i) for i in range(1, count)])

    first[pl.ds(col, 1), :] = part
    out1, in1 = total_moves(0, TILES_Y, col, lambda i: (row * TILES_Y + (col + i) % TILES_Y, slab))
    for move in out1:
        move.start()

    for q in range(2):
        for w in range(WAVES):
            base = 36 * q + 9 * w
            for k in range(4):
                spec[0, base:base + 8, 128 * k:128 * k + 128] = acc[q, w, k]
                spec[0, base + 8:base + 9, 128 * k:128 * k + 128] = acc[q, w, 4, k:k + 1, :]

    for move in moves:
        move.wait_recv()
    magnetic_phase(STEPS - 1)
    for k in range(3):
        stores.append(pltpu.make_async_copy(
            hs.at[k, pl.ds(1, CX), pl.ds(8, CY), :], h_out.at[0, k], local_sem.at[10 + k]))
        stores[-1].start()

    for move in in1:
        move.wait_recv()
    second[pl.ds(row, 1), :] = jnp.sum(first[0:TILES_Y, :], axis=0, keepdims=True)
    out2, in2 = total_moves(1, TILES_X, row, lambda i: ((row + i) % TILES_X * TILES_Y + col, slab))
    for move in out2:
        move.start()
    for move in moves:
        move.wait_send()
    for n in range(STEPS):
        for i in range(1, SLABS):
            plane_move(n, i).wait_send()
    for move in out1:
        move.wait_send()
    for store in stores:
        store.wait()
    for move in in2:
        move.wait_recv()
    for move in out2:
        move.wait_send()
    cells = TILES_X * TILES_Y * WAVES * MON * 3 * CX * CY
    objective[0] = jnp.sum(second[0:TILES_X, :]) / jnp.float32(cells)


def step(e_field, h_field, material, permittivity, pml_x, pml_y, pml_z, monitor_z, omega, focus):
    vmem = lambda *shape: pltpu.VMEM(shape, F32)
    dma = lambda *shape: pltpu.SemaphoreType.DMA(shape)
    anywhere = pl.BlockSpec(memory_space=pl.ANY)
    smem = pl.BlockSpec(memory_space=pltpu.SMEM)
    inside = pl.BlockSpec(memory_space=pltpu.VMEM)
    early = STEPS - 1
    e_out, h_out, spectra, objective = pl.pallas_call(
        kernel,
        out_shape=(
            jax.ShapeDtypeStruct(e_field.shape, F32),
            jax.ShapeDtypeStruct(h_field.shape, F32),
            jax.ShapeDtypeStruct((1, 2 * WAVES * MON * 3, CX * CY), F32),
            jax.ShapeDtypeStruct((1,), F32),
        ),
        in_specs=[anywhere] * 3 + [inside] + [smem] * 6,
        out_specs=(anywhere, anywhere, inside, smem),
        scratch_shapes=[
            vmem(3, CX + 1, CY + 8, CZ), vmem(3, CX + 1, CY + 8, CZ), pltpu.VMEM((CX, CY, CZ), jnp.int32),
            vmem(CX, CY, CZ), vmem(CX, CY, CZ), vmem(CX, CY, CZ), vmem(CX, CY, CZ),
            vmem(CX, 128), vmem(CY, 128),
            vmem(2, WAVES, STEPS, 8, 128), vmem(2, WAVES, 5, 8, 128), vmem(STEPS, SLABS, 40, 128),
            vmem(8, 128), vmem(8, 128),
            vmem(2, CX, 128), vmem(8, 128), vmem(2, CY, 128), vmem(2, CX, 128), vmem(2, 8, 128),
            vmem(2, CX, 128), vmem(8, 128), vmem(2, CY, 128), vmem(2, CX, 128), vmem(8, 128),
            vmem(STEPS, 2, CX, 128), vmem(STEPS, 8, 128),
            vmem(STEPS, 2, CY, 128), vmem(STEPS, 2, CX, 128), vmem(STEPS, 8, 128),
            vmem(early, 3, CX, 128), vmem(early, 2, 8, 128),
            vmem(early, 3, CY, 128), vmem(early, 3, CX, 128), vmem(early, 2, 8, 128),
            vmem(6, early, 8, 128),
            dma(13), dma(STEPS + 1, 12), dma(STEPS + 1, 12),
            dma(STEPS, SLABS), dma(STEPS, SLABS), dma(2, 8), dma(2, 8),
        ],
        compiler_params=pltpu.CompilerParams(
            collective_id=0, has_side_effects=True, vmem_limit_bytes=32 * 1024 * 1024),
    )(e_field, h_field, material, focus, permittivity, pml_x, pml_y, pml_z, monitor_z, omega)
    return e_out, h_out, spectra, objective.reshape(())


def solution(mesh):
    field = P("xy", None, None, None, "gz")
    return jax.shard_map(
        step,
        mesh=mesh,
        in_specs=(field, field, P("xy", None, None, "gz"), P(), P(), P(), P(), P(), P(), P("xy", None)),
        out_specs=(field, field, P("xy", None, None), P()),
        check_vma=False,
    )
```

time: 454 us -> 72.1 us (0.16)
  the two profiles are of different devices: /device:TPU:0 before, /device:TPU:1 now
where the time goes in v1:
time: 72.1 us; the launch traced here: 71.8 us
  Pallas kernels  59.1 us (82%)
  local copies, waits for them, and re-layouts  10.3 us (14%)
  between operations  2.42 us (3%)
    pallas_call x1, Pallas kernels, step(): pl.pallas_call(kernel, out_shape=(jax.ShapeDtypeStruct(e_field.shape, F32...  59.1 us
    unnamed x23, local copies, waits for them, and re-layouts  10.3 us

profile of v1, /device:TPU:1, one launch (start us, length us, event | category | flops | bytes accessed | tf_op | source)
XLA Modules:
  0.0 71.8 jit_solution(13701482772811072392)
XLA Ops:
  0.6 0.0 copy-start
  0.6 1.1 %copy-done = f32[1,3,16,32,128]{4,3,2,1,0:T(8,128)S(1)} copy-done((f32[1,3,16,32,128]{4,3,2,1,0:T(8,128)S(1)}, f32[1,3,16,32,128]{4,3,2,1,0:T(8,128)}, u32[]{:S(2)}) %copy-start) | copy-done | bytes 786456
  1.8 0.0 copy-start.1
  1.8 1.1 %copy-done.1 = f32[1,3,16,32,128]{4,3,2,1,0:T(8,128)S(1)} copy-done((f32[1,3,16,32,128]{4,3,2,1,0:T(8,128)S(1)}, f32[1,3,16,32,128]{4,3,2,1,0:T(8,128)}, u32[]{:S(2)}) %copy-start.1) | copy-done | bytes 786456
  2.9 0.0 copy-start.2
  2.9 0.9 %copy-done.2 = s32[1,16,32,128]{3,2,1,0:T(8,128)S(1)} copy-done((s32[1,16,32,128]{3,2,1,0:T(8,128)S(1)}, s32[1,16,32,128]{3,2,1,0:T(8,128)}, u32[]{:S(2)}) %copy-start.2) | copy-done | bytes 262168
  3.9 0.0 copy-start.3
  3.9 0.7 copy-done.3
  4.5 0.0 copy-start.4
  4.5 0.7 copy-done.4
  5.2 0.0 copy-start.5
  5.2 0.7 copy-done.5
  5.9 0.0 copy-start.6
  5.9 0.7 copy-done.6
  6.6 0.0 copy-start.7
  6.6 0.7 copy-done.7
  7.2 0.0 copy-start.8
  7.2 0.7 copy-done.8
  7.9 0.0 copy-start.9
  7.9 0.7 copy-done.9
  8.5 59.1 %shard_map.129 = (f32[1,3,16,32,128]{4,3,2,1,0:T(8,128)S(1)}, f32[1,3,16,32,128]{4,3,2,1,0:T(8,128)S(1)}, f32[1,72,512]{2,1,0:T(8,128)S(1)}, f32[1]{0:T(128)}) custom-call(f32[1,3,16,32,128]{4,3,2,1,0:T(8,128)S(1)} %copy-done, f32[1,3,16,32,128]{4,3,2,1,0:T(8,128)S(1)} %copy-done.1, s32[1,16,32,128]{3,2,1,0:T(8,128)S(1)} %copy-done.2, ...), custom_call_target="tpu_custom_call" | custom-call | tf_op jit(solution)/shard_map/pallas_call | solution.py:490
  67.6 0.9 %copy.18 = f32[1,3,16,32,128]{4,3,2,1,0:T(8,128)} copy(f32[1,3,16,32,128]{4,3,2,1,0:T(8,128)S(1)} %get-tuple-element.16) | data formatting | bytes 1572864
  68.5 0.9 %copy.19 = f32[1,3,16,32,128]{4,3,2,1,0:T(8,128)} copy(f32[1,3,16,32,128]{4,3,2,1,0:T(8,128)S(1)} %get-tuple-element.17) | data formatting | bytes 1572864
  69.4 0.7 copy.20
Async XLA Ops:
  0.6 1.1 %copy-start = (f32[1,3,16,32,128]{4,3,2,1,0:T(8,128)S(1)}, f32[1,3,16,32,128]{4,3,2,1,0:T(8,128)}, u32[]{:S(2)}) copy-start(f32[1,3,16,32,128]{4,3,2,1,0:T(8,128)} %e_in.1) | copy-start | bytes 2359300
  1.8 1.1 %copy-start.1 = (f32[1,3,16,32,128]{4,3,2,1,0:T(8,128)S(1)}, f32[1,3,16,32,128]{4,3,2,1,0:T(8,128)}, u32[]{:S(2)}) copy-start(f32[1,3,16,32,128]{4,3,2,1,0:T(8,128)} %h_in.1) | copy-start | bytes 2359300
  2.9 0.9 %copy-start.2 = (s32[1,16,32,128]{3,2,1,0:T(8,128)S(1)}, s32[1,16,32,128]{3,2,1,0:T(8,128)}, u32[]{:S(2)}) copy-start(s32[1,16,32,128]{3,2,1,0:T(8,128)} %m_in.1) | copy-start | bytes 786436
  3.9 0.7 copy-start.3
  4.5 0.7 copy-start.4
  5.2 0.7 copy-start.5
  5.9 0.7 copy-start.6
  6.6 0.7 copy-start.7
  7.2 0.7 copy-start.8
  7.9 0.7 copy-start.9

commit v2 on v1

--- a/solution.py
+++ b/solution.py
@@ -45,7 +45,7 @@
     e_in, h_in, m_in, focus, permit, pml_x, pml_y, pml_z, monitor, omega,
     e_out, h_out, spec, objective,
     es, hs, kinds, ca, cb, da, db, grades_x, grades_y, trig, acc, planes, first, second,
-    hy, hz, dax, day, daz,
+    hy, hz, dax, day, daz, dby, dbz,
     s_hy, s_hz, r_hx, r_hy, r_hz,
     s_ey, s_ez, r_ex, r_ey, r_ez,
     s_uy, s_uz, r_ux, r_uy, r_uz, r_edge,
@@ -54,6 +54,7 @@
     tile = lax.axis_index("xy")
     slab = lax.axis_index("gz")
     row, col = tile // TILES_Y, tile % TILES_Y
+    half, core = slab // 2, slab % 2
 
     def valid(off):
         r, c, g = row + off[0], col + off[1], slab + off[2]
@@ -92,12 +93,19 @@
     def greet(where):
         pl.semaphore_signal(barrier, inc=1, device_id=where, device_id_type=MESH)
 
-    for i in range(1, TILES_Y):
-        greet((row * TILES_Y + (col + i) % TILES_Y, slab))
-    for i in range(1, TILES_X):
-        greet(((row + i) % TILES_X * TILES_Y + col, slab))
-    for i in range(1, SLABS):
-        greet((tile, (slab + i) % SLABS))
+    def in_row(i):
+        k = (col * 2 + core + i) % (2 * TILES_Y)
+        return row * TILES_Y + k // 2, half * 2 + k % 2
+
+    def in_column(i):
+        k = (row * 2 + half + i) % (2 * TILES_X)
+        return k // 2 * TILES_Y + col, k % 2 * 2 + core
+
+    for i in range(1, 2 * TILES_Y):
+        greet(in_row(i))
+    for i in range(1, 2 * TILES_X):
+        greet(in_column(i))
+    greet((tile, SLABS - 1 - slab))
     for off in EDGES:
         @pl.when(valid(off))
         def _(off=off):
@@ -149,17 +157,15 @@
     for k in range(3):
         loads[k].wait()
 
-    def pack_h(x, total):
-        total = roll(total, -4, 1)
-        h0 = hs[0, x + 1, 8:8 + CY, :]
-        h1 = hs[1, x + 1, 8:8 + CY, :]
-        s_hy[0, pl.ds(x, 1), :] = h0[CY - 1:CY]
-        s_hy[1, pl.ds(x, 1), :] = hs[2, x + 1, 7 + CY:8 + CY, :]
-        return pack(pack(total, h0, 127, 60), h1, 127, 124)
-
-    s_hz[...] = lax.fori_loop(0, CX, pack_h, zero8)
-
-    greeted = TILES_Y - 1 + TILES_X - 1 + SLABS - 1
+    total = zero8
+    for x in range(CX):
+        s_hy[0, x:x + 1, :] = hs[0, x + 1, 7 + CY:8 + CY, :]
+        s_hy[1, x:x + 1, :] = hs[2, x + 1, 7 + CY:8 + CY, :]
+        total = pack(total, hs[0, x + 1, 8:8 + CY, :], 127, 4 * x)
+        total = pack(total, hs[1, x + 1, 8:8 + CY, :], 127, 64 + 4 * x)
+    s_hz[...] = total
+
+    greeted = 2 * TILES_Y - 1 + 2 * TILES_X - 1 + 1
     for off in EDGES:
         greeted = greeted + jnp.where(valid(off), 1, 0)
     pl.semaphore_wait(barrier, greeted)
@@ -197,6 +203,16 @@
         return 0
 
     lax.fori_loop(0, CX, fill, 0)
+    total = zero8
+    for x in range(CX):
+        dby[x:x + 1, :] = db[x, CY - 1:CY, :]
+        total = pack(total, db[x], 127, 4 * x)
+    dbz[...] = total + roll(total, 64, 1)
+    for k in (1, 2):
+        es[k, CX, 0:CY, :] = jnp.zeros((CY, 128), F32)
+    for x in range(CX):
+        es[0, x, CY:CY + 1, :] = jnp.zeros((1, 128), F32)
+        es[2, x, CY:CY + 1, :] = jnp.zeros((1, 128), F32)
 
     def below(ref, off, sigma):
         inside = jnp.where(valid(off), 1.0, 0.0).astype(F32)
@@ -235,11 +251,13 @@
     for move in opening:
         move.wait_send()
 
-    def electric_phase(n):
-        def body(x, carry):
-            halo, low, high, high2 = carry
-            hs[0, x + 1, 7:8, :] = hy[0, pl.ds(x, 1), :]
-            hs[2, x + 1, 7:8, :] = hy[1, pl.ds(x, 1), :]
+    def electric_planes(n, where, last, packs):
+        for x in where:
+            hs[0, x + 1, 7:8, :] = hy[0, x:x + 1, :]
+            hs[2, x + 1, 7:8, :] = hy[1, x:x + 1, :]
+        halo = hz[...]
+        low, high, high2 = packs
+        for x in where:
             h0 = hs[0, x + 1, 8:8 + CY, :]
             h1 = hs[1, x + 1, 8:8 + CY, :]
             h2 = hs[2, x + 1, 8:8 + CY, :]
@@ -247,8 +265,8 @@
             h2y = hs[2, x + 1, 7:7 + CY, :]
             h1x = hs[1, x, 8:8 + CY, :]
             h2x = hs[2, x, 8:8 + CY, :]
-            h0z = jnp.where(lane32 == 0, unpack(halo, 0, 0), roll(h0, 1, 1))
-            h1z = jnp.where(lane32 == 0, unpack(halo, 64, 0), roll(h1, 1, 1))
+            h0z = jnp.where(lane32 == 0, unpack(halo, 4 * x, 0), roll(h0, 1, 1))
+            h1z = jnp.where(lane32 == 0, unpack(halo, 64 + 4 * x, 0), roll(h1, 1, 1))
             decay, drive = ca[x], cb[x]
             e0 = decay * es[0, x, 0:CY, :] + drive * ((h2 - h2y) - (h1 - h1z))
             e1 = decay * es[1, x, 0:CY, :] + drive * ((h0 - h0z) - (h2 - h2x))
@@ -256,41 +274,41 @@
             es[0, x, 0:CY, :] = e0
             es[1, x, 0:CY, :] = e1
             es[2, x, 0:CY, :] = e2
-            s_ey[n, 0, pl.ds(x, 1), :] = e0[0:1]
-            s_ey[n, 1, pl.ds(x, 1), :] = e2[0:1]
-            low = pack(pack(roll(low, -4, 1), e0, 0, 60), e1, 0, 124)
-            if n < STEPS - 1:
+            s_ey[n, 0, x:x + 1, :] = e0[0:1]
+            s_ey[n, 1, x:x + 1, :] = e2[0:1]
+            low = pack(pack(low, e0, 0, 4 * x), e1, 0, 64 + 4 * x)
+            if not last:
                 for k, e in enumerate((e0, e1, e2)):
-                    s_uy[n, k, pl.ds(x, 1), :] = e[CY - 1:CY]
-                high = pack(pack(roll(high, -4, 1), e0, 127, 60), e1, 127, 124)
-                high2 = pack(pack(roll(high2, -4, 1), e2, 127, 60), e2, 127, 124)
-            return roll(halo, -4, 1), low, high, high2
-
-        _, low, high, high2 = lax.fori_loop(0, CX, body, (hz[...], zero8, zero8, zero8))
-        s_ez[n] = low
-        if n < STEPS - 1:
-            s_uz[n, 0] = high
-            s_uz[n, 1] = high2
-
-    def electric_moves(n):
+                    s_uy[n, k, x:x + 1, :] = e[CY - 1:CY]
+                high = pack(pack(high, e0, 127, 4 * x), e1, 127, 64 + 4 * x)
+                high2 = pack(pack(high2, e2, 127, 4 * x), e2, 127, 64 + 4 * x)
+        return low, high, high2
+
+    def electric_phase(n, last):
+        first_moves = [Move(n, 0, (-1, 0, 0), es.at[pl.ds(1, 2), 0, pl.ds(0, CY), :], r_ex.at[n])]
         moves = [
-            Move(n, 0, (-1, 0, 0), es.at[pl.ds(1, 2), 0, pl.ds(0, CY), :], r_ex.at[n]),
             Move(n, 1, (0, -1, 0), s_ey.at[n], r_ey.at[n]),
             Move(n, 2, (0, 0, -1), s_ez.at[n], r_ez.at[n]),
         ]
-        if n == STEPS - 1:
-            return moves
-        sources = (s_ez.at[n], s_uz.at[n, 1], es.at[0, CX - 1, pl.ds(0, 8), :], es.at[1, 0, pl.ds(CY - 8, 8), :], s_ez.at[n], s_uz.at[n, 1])
-        edges = [Move(n, 6 + k, off, sources[k], r_edge.at[k, n]) for k, off in enumerate(EDGES)]
-        return [
-            edges[2], edges[3],
-            Move(n, 3, (1, 0, 0), es.at[:, CX - 1, pl.ds(0, CY), :], r_ux.at[n]),
-            moves[0],
-            Move(n, 4, (0, 1, 0), s_uy.at[n], r_uy.at[n]),
-            moves[1], edges[0], edges[1], edges[4], edges[5],
-            Move(n, 5, (0, 0, 1), s_uz.at[n], r_uz.at[n]),
-            moves[2],
-        ]
+        if not last:
+            sources = (s_ez.at[n], s_uz.at[n, 1], es.at[0, CX - 1, pl.ds(0, 8), :],
+                       es.at[1, 0, pl.ds(CY - 8, 8), :], s_ez.at[n], s_uz.at[n, 1])
+            edges = [Move(n, 6 + k, off, sources[k], r_edge.at[k, n]) for k, off in enumerate(EDGES)]
+            first_moves = edges[2:4] + [
+                Move(n, 3, (1, 0, 0), es.at[:, CX - 1, pl.ds(0, CY), :], r_ux.at[n])] + first_moves
+            moves = [moves[0], Move(n, 4, (0, 1, 0), s_uy.at[n], r_uy.at[n])] + edges[0:2] + edges[4:6] + [
+                moves[1], Move(n, 5, (0, 0, 1), s_uz.at[n], r_uz.at[n])]
+        packs = electric_planes(n, (0,) if last else (0, CX - 1), last, (zero8, zero8, zero8))
+        for move in first_moves:
+            move.start()
+        low, high, high2 = electric_planes(n, range(1, CX if last else CX - 1), last, packs)
+        s_ez[n] = low
+        if not last:
+            s_uz[n, 0] = high
+            s_uz[n, 1] = high2
+        for move in moves:
+            move.start()
+        return first_moves + moves
 
     def below_phase(n):
         e0, e1, e2 = r_ux[n, 0], r_ux[n, 1], r_ux[n, 2]
@@ -319,13 +337,8 @@
         curl = jnp.where(lane8 < 64, (e2y - e2) - along, along - (e2x - e2))
         hz[...] = daz[0] * hz[...] - daz[1] * curl
 
-    def magnetic_phase(n):
-        es[1, CX, 0:CY, :] = r_ex[n, 0]
-        es[2, CX, 0:CY, :] = r_ex[n, 1]
-
-        def body(x, halo):
-            es[0, x, CY:CY + 1, :] = r_ey[n, 0, pl.ds(x, 1), :]
-            es[2, x, CY:CY + 1, :] = r_ey[n, 1, pl.ds(x, 1), :]
+    def magnetic_phase():
+        for x in range(CX):
             e0 = es[0, x, 0:CY, :]
             e1 = es[1, x, 0:CY, :]
             e2 = es[2, x, 0:CY, :]
@@ -333,15 +346,31 @@
             e2y = es[2, x, 1:1 + CY, :]
             e1x = es[1, x + 1, 0:CY, :]
             e2x = es[2, x + 1, 0:CY, :]
-            e0z = jnp.where(lane32 == 127, unpack(halo, 0, 127), roll(e0, -1, 1))
-            e1z = jnp.where(lane32 == 127, unpack(halo, 64, 127), roll(e1, -1, 1))
+            e0z = jnp.where(lane32 == 127, 0.0, roll(e0, -1, 1))
+            e1z = jnp.where(lane32 == 127, 0.0, roll(e1, -1, 1))
             decay, drive = da[x], db[x]
-            hs[0, x + 1, 8:8 + CY, :] = decay * hs[0, x + 1, 8:8 + CY, :] - drive * ((e2y - e2) - (e1z - e1))
-            hs[1, x + 1, 8:8 + CY, :] = decay * hs[1, x + 1, 8:8 + CY, :] - drive * ((e0z - e0) - (e2x - e2))
-            hs[2, x + 1, 8:8 + CY, :] = decay * hs[2, x + 1, 8:8 + CY, :] - drive * ((e1x - e1) - (e0y - e0))
-            return roll(halo, -4, 1)
-
-        lax.fori_loop(0, CX, body, r_ez[n])
+            h0 = decay * hs[0, x + 1, 8:8 + CY, :] - drive * ((e2y - e2) - (e1z - e1))
+            h1 = decay * hs[1, x + 1, 8:8 + CY, :] - drive * ((e0z - e0) - (e2x - e2))
+            h2 = decay * hs[2, x + 1, 8:8 + CY, :] - drive * ((e1x - e1) - (e0y - e0))
+            hs[0, x + 1, 8:8 + CY, :] = h0
+            hs[1, x + 1, 8:8 + CY, :] = h1
+            hs[2, x + 1, 8:8 + CY, :] = h2
+
+    def above_phase(n):
+        drive = db[CX - 1]
+        hs[1, CX, 8:8 + CY, :] = hs[1, CX, 8:8 + CY, :] + drive * r_ex[n, 1]
+        hs[2, CX, 8:8 + CY, :] = hs[2, CX, 8:8 + CY, :] - drive * r_ex[n, 0]
+        term0 = dby[...] * r_ey[n, 1]
+        term2 = dby[...] * r_ey[n, 0]
+        for x in range(CX):
+            hs[0, x + 1, 7 + CY:8 + CY, :] = hs[0, x + 1, 7 + CY:8 + CY, :] - term0[x:x + 1]
+            hs[2, x + 1, 7 + CY:8 + CY, :] = hs[2, x + 1, 7 + CY:8 + CY, :] + term2[x:x + 1]
+        terms = dbz[...] * r_ez[n]
+        for x in range(CX):
+            hs[0, x + 1, 8:8 + CY, :] = hs[0, x + 1, 8:8 + CY, :] + jnp.where(
+                lane32 == 127, unpack(terms, 64 + 4 * x, 127), 0.0)
+            hs[1, x + 1, 8:8 + CY, :] = hs[1, x + 1, 8:8 + CY, :] - jnp.where(
+                lane32 == 127, unpack(terms, 4 * x, 127), 0.0)
 
     def extract_planes(n):
         weights = []
@@ -349,20 +378,27 @@
             weight = jnp.zeros((16, 128), F32)
             for p in range(MON):
                 weight = jnp.where((row16 == 3 * p + c) & (lane16 + slab * CZ == monitor[p]), 1.0, weight)
-            weights.append(weight.astype(jnp.bfloat16))
+            weights += [weight.astype(jnp.bfloat16)] * 3
+        weights = jnp.concatenate(weights, axis=1)
         planes[n, slab, 32:40, :] = zero8
-
-        for k in range(CX // 4):
-            total = jnp.zeros((16, 128), F32)
+        for k in range(0, CX // 4, 2):
+            pieces = []
             for c in range(3):
-                rest = es[c, 4 * k:4 * k + 4, 0:CY, :].reshape(128, 128)
+                rest = es[c, 4 * k:4 * k + 8, 0:CY, :].reshape(256, 128)
                 for _ in range(3):
-                    piece = rest.astype(jnp.bfloat16)
-                    rest = rest - piece.astype(F32)
-                    total = total + lax.dot_general(
-                        weights[c], piece, (((1,), (1,)), ((), ())), preferred_element_type=F32)
-            planes[n, slab, 8 * k:8 * k + 8, :] = total[0:8]
-            planes[n, slab, 32 + k:33 + k, :] = total[8:9]
+                    pieces.append(rest.astype(jnp.bfloat16))
+                    rest = rest - pieces[-1].astype(F32)
+            total = lax.dot_general(weights, jnp.concatenate(pieces, axis=1), (((1,), (1,)), ((), ())),
+                                    preferred_element_type=F32)
+            for j in range(2):
+                part = total[:, 128 * j:128 * j + 128]
+                planes[n, slab, 8 * (k + j):8 * (k + j) + 8, :] = part[0:8]
+                planes[n, slab, 32 + k + j:33 + k + j, :] = part[8:9]
+        for k in range(5):
+            whole = planes[n, slab, 8 * k:8 * k + 8, :]
+            for q in range(2):
+                for w in range(WAVES):
+                    acc[q, w, k] = acc[q, w, k] + trig[q, w, n] * whole
 
     def plane_move(n, i):
         return pltpu.make_async_remote_copy(
@@ -377,94 +413,98 @@
             send_sem=plane_send.at[n, i - 1], recv_sem=plane_recv.at[n, i - 1],
             device_id=(tile, (slab + i) % SLABS), device_id_type=MESH)
 
-    def accumulate(n):
+    def full_step(n, carry):
+        moves = electric_phase(n, False)
+        extract_planes(n)
+        for i in range(1, SLABS):
+            plane_move(n, i).start()
+        magnetic_phase()
+        for move in moves:
+            move.wait_send()
+        for move in moves:
+            move.wait_recv()
+        above_phase(n)
+        below_phase(n)
+        return carry
+
+    lax.fori_loop(0, STEPS - 1, full_step, 0)
+    moves = electric_phase(STEPS - 1, True)
+    extract_planes(STEPS - 1)
+    for i in range(1, SLABS):
+        plane_move(STEPS - 1, i).start()
+
+    part = jnp.zeros((1, 128), F32)
+    odd = zero8
+    for w in range(WAVES):
+        odd = odd + (acc[0, w, 4] * acc[0, w, 4] + acc[1, w, 4] * acc[1, w, 4])
+    for k in range(4):
+        power = zero8
+        for w in range(WAVES):
+            power = power + (acc[0, w, k] * acc[0, w, k] + acc[1, w, k] * acc[1, w, k])
+        power = jnp.sum(power, axis=0, keepdims=True) + odd[k:k + 1]
+        part = part + power * focus[0:1, 128 * k:128 * k + 128]
+
+    def total_moves(stage, count, mine, where):
+        buf = (first, second)[stage]
+
+        def one(slot, i):
+            return pltpu.make_async_remote_copy(
+                src_ref=buf.at[pl.ds(slot, 1), :], dst_ref=buf.at[pl.ds(slot, 1), :],
+                send_sem=total_send.at[stage, i], recv_sem=total_recv.at[stage, i],
+                device_id=where(i), device_id_type=MESH)
+
+        order = sorted(range(1, count), key=lambda i: -min(i, count - i))
+        return ([one(mine, i) for i in order],
+                [one((mine + count - i) % count, i) for i in order])
+
+    first[pl.ds(col * 2 + core, 1), :] = part
+    out1, in1 = total_moves(0, 2 * TILES_Y, col * 2 + core, in_row)
+    for move in out1:
+        move.start()
+
+    stores = [pltpu.make_async_copy(
+        es.at[k, pl.ds(0, CX), pl.ds(0, CY), :], e_out.at[0, k], local_sem.at[7 + k]) for k in range(3)]
+    for store in stores:
+        store.start()
+    magnetic_phase()
+    for move in moves:
+        move.wait_send()
+    for move in moves:
+        move.wait_recv()
+    above_phase(STEPS - 1)
+    for k in range(3):
+        stores.append(pltpu.make_async_copy(
+            hs.at[k, pl.ds(1, CX), pl.ds(8, CY), :], h_out.at[0, k], local_sem.at[10 + k]))
+        stores[-1].start()
+
+    for move in in1:
+        move.wait_recv()
+    second[pl.ds(row * 2 + half, 1), :] = jnp.sum(first[...], axis=0, keepdims=True)
+    out2, in2 = total_moves(1, 2 * TILES_X, row * 2 + half, in_column)
+    for move in out2:
+        move.start()
+
+    for n in range(STEPS):
         for i in range(1, SLABS):
             plane_arrival(n, i).wait_recv()
-        for k in range(5):
+    for k in range(5):
+        spectrum = [[zero8] * WAVES, [zero8] * WAVES]
+        for n in range(STEPS):
             whole = planes[n, 0, 8 * k:8 * k + 8, :]
             for g in range(1, SLABS):
                 whole = whole + planes[n, g, 8 * k:8 * k + 8, :]
             for q in range(2):
                 for w in range(WAVES):
-                    acc[q, w, k] = acc[q, w, k] + trig[q, w, n] * whole
-
-    for n in range(STEPS):
-        electric_phase(n)
-        moves = electric_moves(n)
-        for move in moves:
-            move.start()
-        extract_planes(n)
-        for i in range(1, SLABS):
-            plane_move(n, i).start()
-        if n == STEPS - 1:
-            break
-        if n:
-            accumulate(n - 1)
-        for move in moves:
-            move.wait_recv()
-        magnetic_phase(n)
-        below_phase(n)
-        for move in moves:
-            move.wait_send()
-
-    stores = [pltpu.make_async_copy(
-        es.at[k, pl.ds(0, CX), pl.ds(0, CY), :], e_out.at[0, k], local_sem.at[7 + k]) for k in range(3)]
-    for store in stores:
-        store.start()
-    accumulate(STEPS - 2)
-    accumulate(STEPS - 1)
-
-    part = jnp.zeros((1, 128), F32)
-    odd = jnp.zeros((8, 128), F32)
-    for w in range(WAVES):
-        odd = odd + (acc[0, w, 4] * acc[0, w, 4] + acc[1, w, 4] * acc[1, w, 4])
-    for k in range(4):
-        power = jnp.zeros((8, 128), F32)
-        for w in range(WAVES):
-            power = power + (acc[0, w, k] * acc[0, w, k] + acc[1, w, k] * acc[1, w, k])
-        power = jnp.sum(power, axis=0, keepdims=True) + odd[k:k + 1]
-        part = part + power * focus[0:1, 128 * k:128 * k + 128]
-
-    def total_moves(stage, count, mine, where):
-        buf = (first, second)[stage]
-
-        def one(slot, i):
-            return pltpu.make_async_remote_copy(
-                src_ref=buf.at[pl.ds(slot, 1), :], dst_ref=buf.at[pl.ds(slot, 1), :],
-                send_sem=total_send.at[stage, i], recv_sem=total_recv.at[stage, i],
-                device_id=where(i), device_id_type=MESH)
-
-        return ([one(mine, i) for i in range(1, count)],
-                [one((mine + count - i) % count, i) for i in range(1, count)])
-
-    first[pl.ds(col, 1), :] = part
-    out1, in1 = total_moves(0, TILES_Y, col, lambda i: (row * TILES_Y + (col + i) % TILES_Y, slab))
-    for move in out1:
-        move.start()
-
-    for q in range(2):
-        for w in range(WAVES):
-            base = 36 * q + 9 * w
-            for k in range(4):
-                spec[0, base:base + 8, 128 * k:128 * k + 128] = acc[q, w, k]
-                spec[0, base + 8:base + 9, 128 * k:128 * k + 128] = acc[q, w, 4, k:k + 1, :]
-
-    for move in moves:
-        move.wait_recv()
-    magnetic_phase(STEPS - 1)
-    for k in range(3):
-        stores.append(pltpu.make_async_copy(
-            hs.at[k, pl.ds(1, CX), pl.ds(8, CY), :], h_out.at[0, k], local_sem.at[10 + k]))
-        stores[-1].start()
-
-    for move in in1:
-        move.wait_recv()
-    second[pl.ds(row, 1), :] = jnp.sum(first[0:TILES_Y, :], axis=0, keepdims=True)
-    out2, in2 = total_moves(1, TILES_X, row, lambda i: ((row + i) % TILES_X * TILES_Y + col, slab))
-    for move in out2:
-        move.start()
-    for move in moves:
-        move.wait_send()
+                    spectrum[q][w] = spectrum[q][w] + trig[q, w, n] * whole
+        for q in range(2):
+            for w in range(WAVES):
+                base = 36 * q + 9 * w
+                if k < 4:
+                    spec[0, base:base + 8, 128 * k:128 * k + 128] = spectrum[q][w]
+                else:
+                    for j in range(4):
+                        spec[0, base + 8:base + 9, 128 * j:128 * j + 128] = spectrum[q][w][j:j + 1]
+
     for n in range(STEPS):
         for i in range(1, SLABS):
             plane_move(n, i).wait_send()
@@ -477,7 +517,22 @@
     for move in out2:
         move.wait_send()
     cells = TILES_X * TILES_Y * WAVES * MON * 3 * CX * CY
-    objective[0] = jnp.sum(second[0:TILES_X, :]) / jnp.float32(cells)
+    objective[0] = jnp.sum(second[...]) / jnp.float32(cells)
+
+
+def hand_on(e_in, h_in, s_in, e_out, h_out, s_out, e_mid, h_mid, s_mid, sem):
+    pieces = [(e_in.at[0, k], e_mid.at[k], e_out.at[0, k]) for k in range(3)]
+    pieces += [(h_in.at[0, k], h_mid.at[k], h_out.at[0, k]) for k in range(3)]
+    pieces += [(s_in, s_mid, s_out)]
+    arrive = [pltpu.make_async_copy(a, b, sem.at[0, k]) for k, (a, b, c) in enumerate(pieces)]
+    leave = [pltpu.make_async_copy(b, c, sem.at[1, k]) for k, (a, b, c) in enumerate(pieces)]
+    for copy in arrive:
+        copy.start()
+    for before, after in zip(arrive, leave):
+        before.wait()
+        after.start()
+    for copy in leave:
+        copy.wait()
 
 
 def step(e_field, h_field, material, permittivity, pml_x, pml_y, pml_z, monitor_z, omega, focus):
@@ -502,8 +557,8 @@
             vmem(CX, CY, CZ), vmem(CX, CY, CZ), vmem(CX, CY, CZ), vmem(CX, CY, CZ),
             vmem(CX, 128), vmem(CY, 128),
             vmem(2, WAVES, STEPS, 8, 128), vmem(2, WAVES, 5, 8, 128), vmem(STEPS, SLABS, 40, 128),
-            vmem(8, 128), vmem(8, 128),
-            vmem(2, CX, 128), vmem(8, 128), vmem(2, CY, 128), vmem(2, CX, 128), vmem(2, 8, 128),
+            vmem(2 * TILES_Y, 128), vmem(2 * TILES_X, 128),
+            vmem(2, CX, 128), vmem(8, 128), vmem(2, CY, 128), vmem(2, CX, 128), vmem(2, 8, 128), vmem(CX, 128), vmem(8, 128),
             vmem(2, CX, 128), vmem(8, 128), vmem(2, CY, 128), vmem(2, CX, 128), vmem(8, 128),
             vmem(STEPS, 2, CX, 128), vmem(STEPS, 8, 128),
             vmem(STEPS, 2, CY, 128), vmem(STEPS, 2, CX, 128), vmem(STEPS, 8, 128),
@@ -511,11 +566,18 @@
             vmem(early, 3, CY, 128), vmem(early, 3, CX, 128), vmem(early, 2, 8, 128),
             vmem(6, early, 8, 128),
             dma(13), dma(STEPS + 1, 12), dma(STEPS + 1, 12),
-            dma(STEPS, SLABS), dma(STEPS, SLABS), dma(2, 8), dma(2, 8),
+            dma(STEPS, SLABS), dma(STEPS, SLABS), dma(2, 16), dma(2, 16),
         ],
         compiler_params=pltpu.CompilerParams(
-            collective_id=0, has_side_effects=True, vmem_limit_bytes=32 * 1024 * 1024),
+            collective_id=0, has_side_effects=True, vmem_limit_bytes=60 * 1024 * 1024),
     )(e_field, h_field, material, focus, permittivity, pml_x, pml_y, pml_z, monitor_z, omega)
+    e_out, h_out, spectra = pl.pallas_call(
+        hand_on,
+        out_shape=tuple(jax.ShapeDtypeStruct(a.shape, F32) for a in (e_out, h_out, spectra)),
+        in_specs=[anywhere] * 3,
+        out_specs=(anywhere,) * 3,
+        scratch_shapes=[vmem(3, CX, CY, CZ), vmem(3, CX, CY, CZ), vmem(1, 72, 512), dma(2, 7)],
+    )(e_out, h_out, spectra)
     return e_out, h_out, spectra, objective.reshape(())
 
 

time: 72.1 us -> 49.2 us (0.68)
  Pallas kernels: 59.1 us -> 46.7 us
  local copies, waits for them, and re-layouts: 10.3 us -> 0 us
    pallas_call x1, Pallas kernels: 59.1 us -> 44.4 us  [step(): pl.pallas_call(kernel, out_shape=(jax.ShapeDtypeStruct(e_field.shape, F32...]
    unnamed x23 -> x0, local copies, waits for them, and re-layouts: 10.3 us -> none
    pallas_call x0 -> x1, Pallas kernels: none -> 2.25 us  [step(): pl.pallas_call(hand_on, out_shape=tuple((jax.ShapeDtypeStruct(a.shape, F3...]
where the time goes in v2:
time: 49.2 us; the launch traced here: 49 us
  Pallas kernels  46.7 us (95%)
  between operations  2.32 us (5%)
    pallas_call x1, Pallas kernels, step(): pl.pallas_call(kernel, out_shape=(jax.ShapeDtypeStruct(e_field.shape, F32...  44.4 us
    pallas_call x1, Pallas kernels, step(): pl.pallas_call(hand_on, out_shape=tuple((jax.ShapeDtypeStruct(a.shape, F3...  2.25 us

profile of v2, /device:TPU:1, one launch (start us, length us, event | category | flops | bytes accessed | tf_op | source)
XLA Modules:
  0.0 49.0 jit_solution(7242204804661597344)
XLA Ops:
  0.6 44.4 %shard_map.129 = (f32[1,3,16,32,128]{4,3,2,1,0:T(8,128)}, f32[1,3,16,32,128]{4,3,2,1,0:T(8,128)}, f32[1,72,512]{2,1,0:T(8,128)}, f32[1]{0:T(128)}) custom-call(f32[1,3,16,32,128]{4,3,2,1,0:T(8,128)} %e_in.1, f32[1,3,16,32,128]{4,3,2,1,0:T(8,128)} %h_in.1, s32[1,16,32,128]{3,2,1,0:T(8,128)} %m_in.1, f32[1,512]{1,0:T(1,128)} %focus.1, f32[4]{0:T(128)} %permit.1, ...), custom_call_target="tpu_custom_call" | custom-call | tf_op jit(solution)/shard_map/pallas_call | solution.py:545
  45.1 2.3 %shard_map.130 = (f32[1,3,16,32,128]{4,3,2,1,0:T(8,128)}, f32[1,3,16,32,128]{4,3,2,1,0:T(8,128)}, f32[1,72,512]{2,1,0:T(8,128)}) custom-call(f32[1,3,16,32,128]{4,3,2,1,0:T(8,128)} %get-tuple-element.11.e_in, f32[1,3,16,32,128]{4,3,2,1,0:T(8,128)} %get-tuple-element.12.h_in, f32[1,72,512]{2,1,0:T(8,128)} %get-tuple-element.13.s_in), custom_call_target="tpu_custom_call" | custom-call | tf_op jit(solution)/shard_map/pallas_call | solution.py:574

commit v3 on v2

--- a/solution.py
+++ b/solution.py
@@ -48,7 +48,7 @@
     hy, hz, dax, day, daz, dby, dbz,
     s_hy, s_hz, r_hx, r_hy, r_hz,
     s_ey, s_ez, r_ex, r_ey, r_ez,
-    s_uy, s_uz, r_ux, r_uy, r_uz, r_edge,
+    s_ux, s_uy, s_uz, s_far, top, r_ux, r_uy, r_uz, r_edge,
     local_sem, send_sem, recv_sem, plane_send, plane_recv, total_send, total_recv,
 ):
     tile = lax.axis_index("xy")
@@ -279,9 +279,14 @@
             low = pack(pack(low, e0, 0, 4 * x), e1, 0, 64 + 4 * x)
             if not last:
                 for k, e in enumerate((e0, e1, e2)):
-                    s_uy[n, k, x:x + 1, :] = e[CY - 1:CY]
+                    top[k, x:x + 1, :] = e[CY - 1:CY]
                 high = pack(pack(high, e0, 127, 4 * x), e1, 127, 64 + 4 * x)
                 high2 = pack(pack(high2, e2, 127, 4 * x), e2, 127, 64 + 4 * x)
+                if x == CX - 1:
+                    e0z = jnp.where(lane32 == 127, 0.0, roll(e0, -1, 1))
+                    e0y = jnp.where(row32 == CY - 1, 0.0, roll(e0, -1, 0))
+                    s_ux[n, 0] = (e0z - e0) + e2
+                    s_ux[n, 1] = (e0 - e0y) - e1
         return low, high, high2
 
     def electric_phase(n, last):
@@ -291,50 +296,55 @@
             Move(n, 2, (0, 0, -1), s_ez.at[n], r_ez.at[n]),
         ]
         if not last:
-            sources = (s_ez.at[n], s_uz.at[n, 1], es.at[0, CX - 1, pl.ds(0, 8), :],
-                       es.at[1, 0, pl.ds(CY - 8, 8), :], s_ez.at[n], s_uz.at[n, 1])
+            sources = (s_ez.at[n], s_far.at[n], es.at[0, CX - 1, pl.ds(0, 8), :],
+                       es.at[1, 0, pl.ds(CY - 8, 8), :], s_ez.at[n], s_far.at[n])
             edges = [Move(n, 6 + k, off, sources[k], r_edge.at[k, n]) for k, off in enumerate(EDGES)]
-            first_moves = edges[2:4] + [
-                Move(n, 3, (1, 0, 0), es.at[:, CX - 1, pl.ds(0, CY), :], r_ux.at[n])] + first_moves
+            first_moves = edges[2:4] + [Move(n, 3, (1, 0, 0), s_ux.at[n], r_ux.at[n])] + first_moves
             moves = [moves[0], Move(n, 4, (0, 1, 0), s_uy.at[n], r_uy.at[n])] + edges[0:2] + edges[4:6] + [
                 moves[1], Move(n, 5, (0, 0, 1), s_uz.at[n], r_uz.at[n])]
+        if n:
+            terms = above_terms(n - 1)
+            above_planes(terms, (0, CX - 2, CX - 1))
         packs = electric_planes(n, (0,) if last else (0, CX - 1), last, (zero8, zero8, zero8))
         for move in first_moves:
             move.start()
+        if n:
+            above_planes(terms, range(1, CX - 2))
         low, high, high2 = electric_planes(n, range(1, CX if last else CX - 1), last, packs)
         s_ez[n] = low
         if not last:
-            s_uz[n, 0] = high
-            s_uz[n, 1] = high2
-        for move in moves:
-            move.start()
-        return first_moves + moves
+            e0, e1, e2 = top[0], top[1], top[2]
+            s_uy[n, 0] = (e1 - jnp.where(lane16 == 127, 0.0, roll(e1, -1, 1))) - e2
+            s_uy[n, 1] = (jnp.where(row16 == CX - 1, 0.0, roll(e1, -1, 0)) - e1) + e0
+            s_far[n] = high2
+            up = roll(high2, -1, 0)
+            e2y = jnp.where(row8 < 7, up, jnp.where(lane8 % 4 == 3, 0.0, roll(up, -1, 1)))
+            e2x = jnp.where(lane8 >= 124, 0.0, roll(high2, -4, 1))
+            e01 = roll(high, 64, 1)
+            s_uz[n] = jnp.where(lane8 < 64, (e2y - high2) + e01, (high2 - e2x) - e01)
+        if not last:
+            for move in moves:
+                move.start()
+        return first_moves, moves
 
     def below_phase(n):
-        e0, e1, e2 = r_ux[n, 0], r_ux[n, 1], r_ux[n, 2]
-        e0z = jnp.where(lane32 == 127, unpack(r_edge[0, n], 60, 127), roll(e0, -1, 1))
-        e0y = jnp.where(row32 == CY - 1, r_edge[2, n, 0:1, :], roll(e0, -1, 0))
-        h1 = hs[1, 0, 8:8 + CY, :]
-        h2 = hs[2, 0, 8:8 + CY, :]
-        hs[1, 0, 8:8 + CY, :] = dax[0] * h1 - dax[1] * ((e0z - e0) - (es[2, 0, 0:CY, :] - e2))
-        hs[2, 0, 8:8 + CY, :] = dax[0] * h2 - dax[1] * ((es[1, 0, 0:CY, :] - e1) - (e0y - e0))
-
-        e0, e1, e2 = r_uy[n, 0], r_uy[n, 1], r_uy[n, 2]
+        curl1 = r_ux[n, 0] + jnp.where(lane32 == 127, unpack(r_edge[0, n], 60, 127), 0.0) - es[2, 0, 0:CY, :]
+        curl2 = r_ux[n, 1] - jnp.where(row32 == CY - 1, r_edge[2, n, 0:1, :], 0.0) + es[1, 0, 0:CY, :]
+        hs[1, 0, 8:8 + CY, :] = dax[0] * hs[1, 0, 8:8 + CY, :] - dax[1] * curl1
+        hs[2, 0, 8:8 + CY, :] = dax[0] * hs[2, 0, 8:8 + CY, :] - dax[1] * curl2
+
         corner = jnp.broadcast_to(r_edge[4, n, 7:8, :], (CX, 128))
         corner = jnp.sum(jnp.where(lane16 == 67 + 4 * row16, corner, 0.0), axis=1, keepdims=True)
-        e1z = jnp.where(lane16 == 127, corner, roll(e1, -1, 1))
-        e1x = jnp.where(row16 == CX - 1, r_edge[3, n, 7:8, :], roll(e1, -1, 0))
-        hy[0] = day[0] * hy[0] - day[1] * ((s_ey[n, 1] - e2) - (e1z - e1))
-        hy[1] = day[0] * hy[1] - day[1] * ((e1x - e1) - (s_ey[n, 0] - e0))
-
-        e2 = r_uz[n, 1]
-        along = roll(s_ez[n] - r_uz[n, 0], 64, 1)
-        up = roll(e2, -1, 0)
-        up_next = roll(up, -1, 1)
+        curl0 = r_uy[n, 0] - jnp.where(lane16 == 127, corner, 0.0) + s_ey[n, 1]
+        curl2 = r_uy[n, 1] + jnp.where(row16 == CX - 1, r_edge[3, n, 7:8, :], 0.0) - s_ey[n, 0]
+        hy[0] = day[0] * hy[0] - day[1] * curl0
+        hy[1] = day[0] * hy[1] - day[1] * curl2
+
+        own = roll(s_ez[n], 64, 1)
         up_edge = roll(roll(r_edge[5, n], -1, 0), 3, 1)
-        e2y = jnp.where(row8 < 7, up, jnp.where(lane8 % 4 == 3, up_edge, up_next))
-        e2x = jnp.where(lane8 >= 124, roll(r_edge[1, n], 124, 1), roll(e2, -4, 1))
-        curl = jnp.where(lane8 < 64, (e2y - e2) - along, along - (e2x - e2))
+        up_edge = jnp.where((row8 == 7) & (lane8 % 4 == 3), up_edge, 0.0) - own
+        far_edge = jnp.where(lane8 >= 124, roll(r_edge[1, n], 124, 1), 0.0) - own
+        curl = r_uz[n] + jnp.where(lane8 < 64, up_edge, -far_edge)
         hz[...] = daz[0] * hz[...] - daz[1] * curl
 
     def magnetic_phase():
@@ -356,21 +366,22 @@
             hs[1, x + 1, 8:8 + CY, :] = h1
             hs[2, x + 1, 8:8 + CY, :] = h2
 
-    def above_phase(n):
-        drive = db[CX - 1]
-        hs[1, CX, 8:8 + CY, :] = hs[1, CX, 8:8 + CY, :] + drive * r_ex[n, 1]
-        hs[2, CX, 8:8 + CY, :] = hs[2, CX, 8:8 + CY, :] - drive * r_ex[n, 0]
-        term0 = dby[...] * r_ey[n, 1]
-        term2 = dby[...] * r_ey[n, 0]
-        for x in range(CX):
+    def above_terms(n):
+        return n, dby[...] * r_ey[n, 1], dby[...] * r_ey[n, 0], dbz[...] * r_ez[n]
+
+    def above_planes(terms, where):
+        n, term0, term2, packed = terms
+        for x in where:
+            if x == CX - 1:
+                hs[1, CX, 8:8 + CY, :] = hs[1, CX, 8:8 + CY, :] + db[x] * r_ex[n, 1]
+                hs[2, CX, 8:8 + CY, :] = hs[2, CX, 8:8 + CY, :] - db[x] * r_ex[n, 0]
             hs[0, x + 1, 7 + CY:8 + CY, :] = hs[0, x + 1, 7 + CY:8 + CY, :] - term0[x:x + 1]
             hs[2, x + 1, 7 + CY:8 + CY, :] = hs[2, x + 1, 7 + CY:8 + CY, :] + term2[x:x + 1]
-        terms = dbz[...] * r_ez[n]
-        for x in range(CX):
-            hs[0, x + 1, 8:8 + CY, :] = hs[0, x + 1, 8:8 + CY, :] + jnp.where(
-                lane32 == 127, unpack(terms, 64 + 4 * x, 127), 0.0)
-            hs[1, x + 1, 8:8 + CY, :] = hs[1, x + 1, 8:8 + CY, :] - jnp.where(
-                lane32 == 127, unpack(terms, 4 * x, 127), 0.0)
+        for x in where:
+            h0 = hs[0, x + 1, 8:8 + CY, :] + jnp.where(lane32 == 127, unpack(packed, 64 + 4 * x, 127), 0.0)
+            h1 = hs[1, x + 1, 8:8 + CY, :] - jnp.where(lane32 == 127, unpack(packed, 4 * x, 127), 0.0)
+            hs[0, x + 1, 8:8 + CY, :] = h0
+            hs[1, x + 1, 8:8 + CY, :] = h1
 
     def extract_planes(n):
         weights = []
@@ -380,7 +391,7 @@
                 weight = jnp.where((row16 == 3 * p + c) & (lane16 + slab * CZ == monitor[p]), 1.0, weight)
             weights += [weight.astype(jnp.bfloat16)] * 3
         weights = jnp.concatenate(weights, axis=1)
-        planes[n, slab, 32:40, :] = zero8
+        planes[slab, n, 32:40, :] = zero8
         for k in range(0, CX // 4, 2):
             pieces = []
             for c in range(3):
@@ -392,46 +403,32 @@
                                     preferred_element_type=F32)
             for j in range(2):
                 part = total[:, 128 * j:128 * j + 128]
-                planes[n, slab, 8 * (k + j):8 * (k + j) + 8, :] = part[0:8]
-                planes[n, slab, 32 + k + j:33 + k + j, :] = part[8:9]
+                planes[slab, n, 8 * (k + j):8 * (k + j) + 8, :] = part[0:8]
+                planes[slab, n, 32 + k + j:33 + k + j, :] = part[8:9]
         for k in range(5):
-            whole = planes[n, slab, 8 * k:8 * k + 8, :]
+            whole = planes[slab, n, 8 * k:8 * k + 8, :]
             for q in range(2):
                 for w in range(WAVES):
                     acc[q, w, k] = acc[q, w, k] + trig[q, w, n] * whole
 
-    def plane_move(n, i):
+    def plane_move(i, source):
         return pltpu.make_async_remote_copy(
-            src_ref=planes.at[n, slab], dst_ref=planes.at[n, slab],
-            send_sem=plane_send.at[n, i - 1], recv_sem=plane_recv.at[n, i - 1],
+            src_ref=planes.at[source], dst_ref=planes.at[source],
+            send_sem=plane_send.at[i - 1], recv_sem=plane_recv.at[i - 1],
             device_id=(tile, (slab + i) % SLABS), device_id_type=MESH)
 
-    def plane_arrival(n, i):
-        source = (slab + SLABS - i) % SLABS
-        return pltpu.make_async_remote_copy(
-            src_ref=planes.at[n, source], dst_ref=planes.at[n, source],
-            send_sem=plane_send.at[n, i - 1], recv_sem=plane_recv.at[n, i - 1],
-            device_id=(tile, (slab + i) % SLABS), device_id_type=MESH)
-
-    def full_step(n, carry):
-        moves = electric_phase(n, False)
+    for n in range(STEPS - 1):
+        moves = sum(electric_phase(n, False), [])
         extract_planes(n)
-        for i in range(1, SLABS):
-            plane_move(n, i).start()
         magnetic_phase()
         for move in moves:
             move.wait_send()
-        for move in moves:
+        for move in reversed(moves):
             move.wait_recv()
-        above_phase(n)
         below_phase(n)
-        return carry
-
-    lax.fori_loop(0, STEPS - 1, full_step, 0)
-    moves = electric_phase(STEPS - 1, True)
+
+    moves, later = electric_phase(STEPS - 1, True)
     extract_planes(STEPS - 1)
-    for i in range(1, SLABS):
-        plane_move(STEPS - 1, i).start()
 
     part = jnp.zeros((1, 128), F32)
     odd = zero8
@@ -444,23 +441,27 @@
         power = jnp.sum(power, axis=0, keepdims=True) + odd[k:k + 1]
         part = part + power * focus[0:1, 128 * k:128 * k + 128]
 
-    def total_moves(stage, count, mine, where):
+    def send_totals(stage, mine, where):
         buf = (first, second)[stage]
-
-        def one(slot, i):
-            return pltpu.make_async_remote_copy(
-                src_ref=buf.at[pl.ds(slot, 1), :], dst_ref=buf.at[pl.ds(slot, 1), :],
-                send_sem=total_send.at[stage, i], recv_sem=total_recv.at[stage, i],
-                device_id=where(i), device_id_type=MESH)
-
-        order = sorted(range(1, count), key=lambda i: -min(i, count - i))
-        return ([one(mine, i) for i in order],
-                [one((mine + count - i) % count, i) for i in order])
+        for i in sorted(range(1, 16), key=lambda i: -min(i, 16 - i)):
+            pltpu.make_async_remote_copy(
+                src_ref=buf.at[pl.ds(mine, 1), :], dst_ref=buf.at[pl.ds(mine, 1), :],
+                send_sem=total_send.at[stage], recv_sem=total_recv.at[stage],
+                device_id=where(i), device_id_type=MESH).start()
+
+    def all_totals(stage):
+        buf = (first, second)[stage].at[pl.ds(0, 15), :]
+        return pltpu.make_async_remote_copy(
+            src_ref=buf, dst_ref=buf, send_sem=total_send.at[stage], recv_sem=total_recv.at[stage],
+            device_id=(in_row, in_column)[stage](1), device_id_type=MESH)
 
     first[pl.ds(col * 2 + core, 1), :] = part
-    out1, in1 = total_moves(0, 2 * TILES_Y, col * 2 + core, in_row)
-    for move in out1:
+    send_totals(0, col * 2 + core, in_row)
+    for move in later:
         move.start()
+    for i in range(1, SLABS):
+        plane_move(i, slab).start()
+    moves = moves + later
 
     stores = [pltpu.make_async_copy(
         es.at[k, pl.ds(0, CX), pl.ds(0, CY), :], e_out.at[0, k], local_sem.at[7 + k]) for k in range(3)]
@@ -469,30 +470,26 @@
     magnetic_phase()
     for move in moves:
         move.wait_send()
-    for move in moves:
+    for move in reversed(moves):
         move.wait_recv()
-    above_phase(STEPS - 1)
+    above_planes(above_terms(STEPS - 1), range(CX))
     for k in range(3):
         stores.append(pltpu.make_async_copy(
             hs.at[k, pl.ds(1, CX), pl.ds(8, CY), :], h_out.at[0, k], local_sem.at[10 + k]))
         stores[-1].start()
 
-    for move in in1:
-        move.wait_recv()
+    all_totals(0).wait_recv()
     second[pl.ds(row * 2 + half, 1), :] = jnp.sum(first[...], axis=0, keepdims=True)
-    out2, in2 = total_moves(1, 2 * TILES_X, row * 2 + half, in_column)
-    for move in out2:
-        move.start()
-
-    for n in range(STEPS):
-        for i in range(1, SLABS):
-            plane_arrival(n, i).wait_recv()
+    send_totals(1, row * 2 + half, in_column)
+
+    for i in range(1, SLABS):
+        plane_move(i, (slab + SLABS - i) % SLABS).wait_recv()
     for k in range(5):
         spectrum = [[zero8] * WAVES, [zero8] * WAVES]
         for n in range(STEPS):
-            whole = planes[n, 0, 8 * k:8 * k + 8, :]
+            whole = planes[0, n, 8 * k:8 * k + 8, :]
             for g in range(1, SLABS):
-                whole = whole + planes[n, g, 8 * k:8 * k + 8, :]
+                whole = whole + planes[g, n, 8 * k:8 * k + 8, :]
             for q in range(2):
                 for w in range(WAVES):
                     spectrum[q][w] = spectrum[q][w] + trig[q, w, n] * whole
@@ -505,17 +502,12 @@
                     for j in range(4):
                         spec[0, base + 8:base + 9, 128 * j:128 * j + 128] = spectrum[q][w][j:j + 1]
 
-    for n in range(STEPS):
-        for i in range(1, SLABS):
-            plane_move(n, i).wait_send()
-    for move in out1:
-        move.wait_send()
+    for i in range(1, SLABS):
+        plane_move(i, slab).wait_send()
+    all_totals(0).wait_send()
     for store in stores:
         store.wait()
-    for move in in2:
-        move.wait_recv()
-    for move in out2:
-        move.wait_send()
+    all_totals(1).wait()
     cells = TILES_X * TILES_Y * WAVES * MON * 3 * CX * CY
     objective[0] = jnp.sum(second[...]) / jnp.float32(cells)
 
@@ -556,17 +548,17 @@
             vmem(3, CX + 1, CY + 8, CZ), vmem(3, CX + 1, CY + 8, CZ), pltpu.VMEM((CX, CY, CZ), jnp.int32),
             vmem(CX, CY, CZ), vmem(CX, CY, CZ), vmem(CX, CY, CZ), vmem(CX, CY, CZ),
             vmem(CX, 128), vmem(CY, 128),
-            vmem(2, WAVES, STEPS, 8, 128), vmem(2, WAVES, 5, 8, 128), vmem(STEPS, SLABS, 40, 128),
+            vmem(2, WAVES, STEPS, 8, 128), vmem(2, WAVES, 5, 8, 128), vmem(SLABS, STEPS, 40, 128),
             vmem(2 * TILES_Y, 128), vmem(2 * TILES_X, 128),
             vmem(2, CX, 128), vmem(8, 128), vmem(2, CY, 128), vmem(2, CX, 128), vmem(2, 8, 128), vmem(CX, 128), vmem(8, 128),
             vmem(2, CX, 128), vmem(8, 128), vmem(2, CY, 128), vmem(2, CX, 128), vmem(8, 128),
             vmem(STEPS, 2, CX, 128), vmem(STEPS, 8, 128),
             vmem(STEPS, 2, CY, 128), vmem(STEPS, 2, CX, 128), vmem(STEPS, 8, 128),
-            vmem(early, 3, CX, 128), vmem(early, 2, 8, 128),
-            vmem(early, 3, CY, 128), vmem(early, 3, CX, 128), vmem(early, 2, 8, 128),
+            vmem(early, 2, CY, 128), vmem(early, 2, CX, 128), vmem(early, 8, 128), vmem(early, 8, 128), vmem(3, CX, 128),
+            vmem(early, 2, CY, 128), vmem(early, 2, CX, 128), vmem(early, 8, 128),
             vmem(6, early, 8, 128),
             dma(13), dma(STEPS + 1, 12), dma(STEPS + 1, 12),
-            dma(STEPS, SLABS), dma(STEPS, SLABS), dma(2, 16), dma(2, 16),
+            dma(SLABS), dma(SLABS), dma(2), dma(2),
         ],
         compiler_params=pltpu.CompilerParams(
             collective_id=0, has_side_effects=True, vmem_limit_bytes=60 * 1024 * 1024),

time: 49.2 us -> 47.2 us (0.959)
  Pallas kernels: 46.7 us -> 44.7 us
    pallas_call x1, Pallas kernels: 44.4 us -> 42.4 us  [step(): pl.pallas_call(kernel, out_shape=(jax.ShapeDtypeStruct(e_field.shape, F32...]
where the time goes in v3:
time: 47.2 us; the launch traced here: 47 us
  Pallas kernels  44.7 us (95%)
  between operations  2.32 us (5%)
    pallas_call x1, Pallas kernels, step(): pl.pallas_call(kernel, out_shape=(jax.ShapeDtypeStruct(e_field.shape, F32...  42.4 us
    pallas_call x1, Pallas kernels, step(): pl.pallas_call(hand_on, out_shape=tuple((jax.ShapeDtypeStruct(a.shape, F3...  2.25 us

profile of v3, /device:TPU:1, one launch (start us, length us, event | category | flops | bytes accessed | tf_op | source)
XLA Modules:
  0.0 47.0 jit_solution(255963322225598226)
XLA Ops:
  0.6 42.4 %shard_map.129 = (f32[1,3,16,32,128]{4,3,2,1,0:T(8,128)}, f32[1,3,16,32,128]{4,3,2,1,0:T(8,128)}, f32[1,72,512]{2,1,0:T(8,128)}, f32[1]{0:T(128)}) custom-call(f32[1,3,16,32,128]{4,3,2,1,0:T(8,128)} %e_in.1, f32[1,3,16,32,128]{4,3,2,1,0:T(8,128)} %h_in.1, s32[1,16,32,128]{3,2,1,0:T(8,128)} %m_in.1, f32[1,512]{1,0:T(1,128)} %focus.1, f32[4]{0:T(128)} %permit.1, ...), custom_call_target="tpu_custom_call" | custom-call | tf_op jit(solution)/shard_map/pallas_call | solution.py:537
  43.0 2.3 %shard_map.130 = (f32[1,3,16,32,128]{4,3,2,1,0:T(8,128)}, f32[1,3,16,32,128]{4,3,2,1,0:T(8,128)}, f32[1,72,512]{2,1,0:T(8,128)}) custom-call(f32[1,3,16,32,128]{4,3,2,1,0:T(8,128)} %get-tuple-element.11.e_in, f32[1,3,16,32,128]{4,3,2,1,0:T(8,128)} %get-tuple-element.12.h_in, f32[1,72,512]{2,1,0:T(8,128)} %get-tuple-element.13.s_in), custom_call_target="tpu_custom_call" | custom-call | tf_op jit(solution)/shard_map/pallas_call | solution.py:566

commit v4 on v3

--- a/solution.py
+++ b/solution.py
@@ -42,14 +42,15 @@
 
 
 def kernel(
-    e_in, h_in, m_in, focus, permit, pml_x, pml_y, pml_z, monitor, omega,
-    e_out, h_out, spec, objective,
+    e_in, h_in, m_in, focus_in, permit_in, pml_x_in, pml_y_in, pml_z_in, monitor_in, omega_in,
+    e_out, h_out, spec_out, objective_out,
+    focus, permit, pml_x, pml_y, pml_z, monitor, omega, spec, objective,
     es, hs, kinds, ca, cb, da, db, grades_x, grades_y, trig, acc, planes, first, second,
     hy, hz, dax, day, daz, dby, dbz,
     s_hy, s_hz, r_hx, r_hy, r_hz,
     s_ey, s_ez, r_ex, r_ey, r_ez,
     s_ux, s_uy, s_uz, s_far, top, r_ux, r_uy, r_uz, r_edge,
-    local_sem, send_sem, recv_sem, plane_send, plane_recv, total_send, total_recv,
+    local_sem, small_sem, send_sem, recv_sem, plane_send, plane_recv, total_send, total_recv,
 ):
     tile = lax.axis_index("xy")
     slab = lax.axis_index("gz")
@@ -121,6 +122,11 @@
             e_in.at[0, k], es.at[k, pl.ds(0, CX), pl.ds(0, CY), :], local_sem.at[4 + k]))
     for load in loads:
         load.start()
+    small = [pltpu.make_async_copy(source, target, small_sem.at[k]) for k, (source, target) in enumerate((
+        (pml_x_in, pml_x), (pml_y_in, pml_y), (pml_z_in, pml_z), (permit_in, permit),
+        (omega_in, omega), (monitor_in, monitor), (focus_in, focus)))]
+    for load in small:
+        load.start()
 
     lane8 = lax.broadcasted_iota(jnp.int32, (8, 128), 1)
     row8 = lax.broadcasted_iota(jnp.int32, (8, 128), 0)
@@ -178,6 +184,8 @@
     for move in opening:
         move.start()
 
+    for load in small:
+        load.wait()
     for i in range(CX):
         grades_x[i:i + 1, :] = jnp.full((1, 128), grade(pml_x[row * CX + i]), F32)
     for j in range(CY):
@@ -502,20 +510,26 @@
                     for j in range(4):
                         spec[0, base + 8:base + 9, 128 * j:128 * j + 128] = spectrum[q][w][j:j + 1]
 
+    stores.append(pltpu.make_async_copy(spec, spec_out, small_sem.at[7]))
+    stores[-1].start()
     for i in range(1, SLABS):
         plane_move(i, slab).wait_send()
     all_totals(0).wait_send()
     for store in stores:
         store.wait()
-    all_totals(1).wait()
+    all_totals(1).wait_recv()
     cells = TILES_X * TILES_Y * WAVES * MON * 3 * CX * CY
     objective[0] = jnp.sum(second[...]) / jnp.float32(cells)
-
-
-def hand_on(e_in, h_in, s_in, e_out, h_out, s_out, e_mid, h_mid, s_mid, sem):
+    result = pltpu.make_async_copy(objective, objective_out, small_sem.at[8])
+    result.start()
+    all_totals(1).wait_send()
+    result.wait()
+
+
+def hand_on(e_in, h_in, s_in, o_in, e_out, h_out, s_out, o_out, e_mid, h_mid, s_mid, o_mid, sem):
     pieces = [(e_in.at[0, k], e_mid.at[k], e_out.at[0, k]) for k in range(3)]
     pieces += [(h_in.at[0, k], h_mid.at[k], h_out.at[0, k]) for k in range(3)]
-    pieces += [(s_in, s_mid, s_out)]
+    pieces += [(s_in, s_mid, s_out), (o_in, o_mid, o_out)]
     arrive = [pltpu.make_async_copy(a, b, sem.at[0, k]) for k, (a, b, c) in enumerate(pieces)]
     leave = [pltpu.make_async_copy(b, c, sem.at[1, k]) for k, (a, b, c) in enumerate(pieces)]
     for copy in arrive:
@@ -531,8 +545,6 @@
     vmem = lambda *shape: pltpu.VMEM(shape, F32)
     dma = lambda *shape: pltpu.SemaphoreType.DMA(shape)
     anywhere = pl.BlockSpec(memory_space=pl.ANY)
-    smem = pl.BlockSpec(memory_space=pltpu.SMEM)
-    inside = pl.BlockSpec(memory_space=pltpu.VMEM)
     early = STEPS - 1
     e_out, h_out, spectra, objective = pl.pallas_call(
         kernel,
@@ -540,11 +552,15 @@
             jax.ShapeDtypeStruct(e_field.shape, F32),
             jax.ShapeDtypeStruct(h_field.shape, F32),
             jax.ShapeDtypeStruct((1, 2 * WAVES * MON * 3, CX * CY), F32),
-            jax.ShapeDtypeStruct((1,), F32),
+            pltpu.SMEM((1,), F32),
         ),
-        in_specs=[anywhere] * 3 + [inside] + [smem] * 6,
-        out_specs=(anywhere, anywhere, inside, smem),
+        in_specs=[anywhere] * 10,
+        out_specs=(anywhere,) * 4,
         scratch_shapes=[
+            vmem(*focus.shape), pltpu.SMEM(permittivity.shape, F32), pltpu.SMEM(pml_x.shape, jnp.int32),
+            pltpu.SMEM(pml_y.shape, jnp.int32), pltpu.SMEM(pml_z.shape, jnp.int32),
+            pltpu.SMEM(monitor_z.shape, jnp.int32), pltpu.SMEM(omega.shape, F32),
+            vmem(1, 2 * WAVES * MON * 3, CX * CY), pltpu.SMEM((1,), F32),
             vmem(3, CX + 1, CY + 8, CZ), vmem(3, CX + 1, CY + 8, CZ), pltpu.VMEM((CX, CY, CZ), jnp.int32),
             vmem(CX, CY, CZ), vmem(CX, CY, CZ), vmem(CX, CY, CZ), vmem(CX, CY, CZ),
             vmem(CX, 128), vmem(CY, 128),
@@ -557,19 +573,20 @@
             vmem(early, 2, CY, 128), vmem(early, 2, CX, 128), vmem(early, 8, 128), vmem(early, 8, 128), vmem(3, CX, 128),
             vmem(early, 2, CY, 128), vmem(early, 2, CX, 128), vmem(early, 8, 128),
             vmem(6, early, 8, 128),
-            dma(13), dma(STEPS + 1, 12), dma(STEPS + 1, 12),
+            dma(13), dma(9), dma(STEPS + 1, 12), dma(STEPS + 1, 12),
             dma(SLABS), dma(SLABS), dma(2), dma(2),
         ],
         compiler_params=pltpu.CompilerParams(
             collective_id=0, has_side_effects=True, vmem_limit_bytes=60 * 1024 * 1024),
     )(e_field, h_field, material, focus, permittivity, pml_x, pml_y, pml_z, monitor_z, omega)
-    e_out, h_out, spectra = pl.pallas_call(
+    results = (e_out, h_out, spectra, objective)
+    e_out, h_out, spectra, objective = pl.pallas_call(
         hand_on,
-        out_shape=tuple(jax.ShapeDtypeStruct(a.shape, F32) for a in (e_out, h_out, spectra)),
-        in_specs=[anywhere] * 3,
-        out_specs=(anywhere,) * 3,
-        scratch_shapes=[vmem(3, CX, CY, CZ), vmem(3, CX, CY, CZ), vmem(1, 72, 512), dma(2, 7)],
-    )(e_out, h_out, spectra)
+        out_shape=tuple(jax.ShapeDtypeStruct(a.shape, F32) for a in results),
+        in_specs=[anywhere] * 4,
+        out_specs=(anywhere,) * 4,
+        scratch_shapes=[vmem(3, CX, CY, CZ), vmem(3, CX, CY, CZ), vmem(*spectra.shape), pltpu.SMEM((1,), F32), dma(2, 8)],
+    )(*results)
     return e_out, h_out, spectra, objective.reshape(())
 
 

time: 47.2 us -> 44.4 us (0.941)
  between operations: 2.32 us -> 0.64 us
  Pallas kernels: 44.7 us -> 43.7 us
    pallas_call x1, Pallas kernels: 42.4 us -> 41.4 us  [step(): pl.pallas_call(kernel, out_shape=(jax.ShapeDtypeStruct(e_field.shape, F32...]
where the time goes in v4:
time: 44.4 us; the launch traced here: 44.3 us
  Pallas kernels  43.7 us (98%)
  between operations  0.64 us (1%)
    pallas_call x1, Pallas kernels, step(): pl.pallas_call(kernel, out_shape=(jax.ShapeDtypeStruct(e_field.shape, F32...  41.4 us
    pallas_call x1, Pallas kernels, step(): pl.pallas_call(hand_on, out_shape=tuple((jax.ShapeDtypeStruct(a.shape, F3...  2.28 us

profile of v4, /device:TPU:1, one launch (start us, length us, event | category | flops | bytes accessed | tf_op | source)
XLA Modules:
  0.0 44.3 jit_solution(4786236275037035156)
XLA Ops:
  0.6 41.4 %shard_map.129 = (f32[1,3,16,32,128]{4,3,2,1,0:T(8,128)}, f32[1,3,16,32,128]{4,3,2,1,0:T(8,128)}, f32[1,72,512]{2,1,0:T(8,128)}, f32[1]{0:T(128)S(4)}) custom-call(f32[1,3,16,32,128]{4,3,2,1,0:T(8,128)} %e_in.1, f32[1,3,16,32,128]{4,3,2,1,0:T(8,128)} %h_in.1, s32[1,16,32,128]{3,2,1,0:T(8,128)} %m_in.1, f32[1,512]{1,0:T(1,128)} %focus_in.1, f32[4]{0:T(128)} %permit_in.1, ...), custom_call_target="tpu_custom_call" | custom-call | tf_op jit(solution)/shard_map/pallas_call | solution.py:549
  42.0 2.3 %shard_map.130 = (f32[1,3,16,32,128]{4,3,2,1,0:T(8,128)}, f32[1,3,16,32,128]{4,3,2,1,0:T(8,128)}, f32[1,72,512]{2,1,0:T(8,128)}, f32[1]{0:T(128)}) custom-call(f32[1,3,16,32,128]{4,3,2,1,0:T(8,128)} %get-tuple-element.12.e_in, f32[1,3,16,32,128]{4,3,2,1,0:T(8,128)} %get-tuple-element.13.h_in, f32[1,72,512]{2,1,0:T(8,128)} %get-tuple-element.14.s_in, ...), custom_call_target="tpu_custom_call" | custom-call | tf_op jit(solution)/shard_map/pallas_call | solution.py:583

commit v5 on v4

--- a/solution.py
+++ b/solution.py
@@ -44,7 +44,7 @@
 def kernel(
     e_in, h_in, m_in, focus_in, permit_in, pml_x_in, pml_y_in, pml_z_in, monitor_in, omega_in,
     e_out, h_out, spec_out, objective_out,
-    focus, permit, pml_x, pml_y, pml_z, monitor, omega, spec, objective,
+    focus, permit, pml_x, pml_y, pml_z, monitor, omega, spec,
     es, hs, kinds, ca, cb, da, db, grades_x, grades_y, trig, acc, planes, first, second,
     hy, hz, dax, day, daz, dby, dbz,
     s_hy, s_hz, r_hx, r_hy, r_hz,
@@ -310,14 +310,9 @@
             first_moves = edges[2:4] + [Move(n, 3, (1, 0, 0), s_ux.at[n], r_ux.at[n])] + first_moves
             moves = [moves[0], Move(n, 4, (0, 1, 0), s_uy.at[n], r_uy.at[n])] + edges[0:2] + edges[4:6] + [
                 moves[1], Move(n, 5, (0, 0, 1), s_uz.at[n], r_uz.at[n])]
-        if n:
-            terms = above_terms(n - 1)
-            above_planes(terms, (0, CX - 2, CX - 1))
         packs = electric_planes(n, (0,) if last else (0, CX - 1), last, (zero8, zero8, zero8))
         for move in first_moves:
             move.start()
-        if n:
-            above_planes(terms, range(1, CX - 2))
         low, high, high2 = electric_planes(n, range(1, CX if last else CX - 1), last, packs)
         s_ez[n] = low
         if not last:
@@ -374,22 +369,27 @@
             hs[1, x + 1, 8:8 + CY, :] = h1
             hs[2, x + 1, 8:8 + CY, :] = h2
 
-    def above_terms(n):
-        return n, dby[...] * r_ey[n, 1], dby[...] * r_ey[n, 0], dbz[...] * r_ez[n]
-
-    def above_planes(terms, where):
-        n, term0, term2, packed = terms
-        for x in where:
-            if x == CX - 1:
-                hs[1, CX, 8:8 + CY, :] = hs[1, CX, 8:8 + CY, :] + db[x] * r_ex[n, 1]
-                hs[2, CX, 8:8 + CY, :] = hs[2, CX, 8:8 + CY, :] - db[x] * r_ex[n, 0]
+    def arrivals(n, moves):
+        for move in moves:
+            move.wait_send()
+        for move in moves:
+            if move.off[0] == 0:
+                move.wait_recv()
+        term0, term2, packed = dby[...] * r_ey[n, 1], dby[...] * r_ey[n, 0], dbz[...] * r_ez[n]
+        for x in range(CX):
             hs[0, x + 1, 7 + CY:8 + CY, :] = hs[0, x + 1, 7 + CY:8 + CY, :] - term0[x:x + 1]
             hs[2, x + 1, 7 + CY:8 + CY, :] = hs[2, x + 1, 7 + CY:8 + CY, :] + term2[x:x + 1]
-        for x in where:
+        for x in range(CX):
             h0 = hs[0, x + 1, 8:8 + CY, :] + jnp.where(lane32 == 127, unpack(packed, 64 + 4 * x, 127), 0.0)
             h1 = hs[1, x + 1, 8:8 + CY, :] - jnp.where(lane32 == 127, unpack(packed, 4 * x, 127), 0.0)
             hs[0, x + 1, 8:8 + CY, :] = h0
             hs[1, x + 1, 8:8 + CY, :] = h1
+        for move in reversed(moves):
+            if move.off[0] != 0:
+                move.wait_recv()
+        drive = db[CX - 1]
+        hs[1, CX, 8:8 + CY, :] = hs[1, CX, 8:8 + CY, :] + drive * r_ex[n, 1]
+        hs[2, CX, 8:8 + CY, :] = hs[2, CX, 8:8 + CY, :] - drive * r_ex[n, 0]
 
     def extract_planes(n):
         weights = []
@@ -429,10 +429,7 @@
         moves = sum(electric_phase(n, False), [])
         extract_planes(n)
         magnetic_phase()
-        for move in moves:
-            move.wait_send()
-        for move in reversed(moves):
-            move.wait_recv()
+        arrivals(n, moves)
         below_phase(n)
 
     moves, later = electric_phase(STEPS - 1, True)
@@ -476,11 +473,7 @@
     for store in stores:
         store.start()
     magnetic_phase()
-    for move in moves:
-        move.wait_send()
-    for move in reversed(moves):
-        move.wait_recv()
-    above_planes(above_terms(STEPS - 1), range(CX))
+    arrivals(STEPS - 1, moves)
     for k in range(3):
         stores.append(pltpu.make_async_copy(
             hs.at[k, pl.ds(1, CX), pl.ds(8, CY), :], h_out.at[0, k], local_sem.at[10 + k]))
@@ -519,25 +512,18 @@
         store.wait()
     all_totals(1).wait_recv()
     cells = TILES_X * TILES_Y * WAVES * MON * 3 * CX * CY
-    objective[0] = jnp.sum(second[...]) / jnp.float32(cells)
-    result = pltpu.make_async_copy(objective, objective_out, small_sem.at[8])
-    result.start()
+    objective_out[0] = jnp.sum(second[...]) / jnp.float32(cells)
     all_totals(1).wait_send()
-    result.wait()
-
-
-def hand_on(e_in, h_in, s_in, o_in, e_out, h_out, s_out, o_out, e_mid, h_mid, s_mid, o_mid, sem):
-    pieces = [(e_in.at[0, k], e_mid.at[k], e_out.at[0, k]) for k in range(3)]
-    pieces += [(h_in.at[0, k], h_mid.at[k], h_out.at[0, k]) for k in range(3)]
-    pieces += [(s_in, s_mid, s_out), (o_in, o_mid, o_out)]
-    arrive = [pltpu.make_async_copy(a, b, sem.at[0, k]) for k, (a, b, c) in enumerate(pieces)]
-    leave = [pltpu.make_async_copy(b, c, sem.at[1, k]) for k, (a, b, c) in enumerate(pieces)]
-    for copy in arrive:
+
+
+def hand_on(e_in, h_in, s_in, o_in, e_out, h_out, s_out, o_out, sem):
+    pieces = [(e_in.at[0, k], e_out.at[0, k]) for k in range(3)]
+    pieces += [(h_in.at[0, k], h_out.at[0, k]) for k in range(3)]
+    pieces += [(s_in, s_out), (o_in, o_out)]
+    copies = [pltpu.make_async_copy(a, b, sem.at[k]) for k, (a, b) in enumerate(pieces)]
+    for copy in copies:
         copy.start()
-    for before, after in zip(arrive, leave):
-        before.wait()
-        after.start()
-    for copy in leave:
+    for copy in copies:
         copy.wait()
 
 
@@ -549,18 +535,18 @@
     e_out, h_out, spectra, objective = pl.pallas_call(
         kernel,
         out_shape=(
-            jax.ShapeDtypeStruct(e_field.shape, F32),
-            jax.ShapeDtypeStruct(h_field.shape, F32),
-            jax.ShapeDtypeStruct((1, 2 * WAVES * MON * 3, CX * CY), F32),
+            pltpu.VMEM(e_field.shape, F32),
+            pltpu.VMEM(h_field.shape, F32),
+            pltpu.VMEM((1, 2 * WAVES * MON * 3, CX * CY), F32),
             pltpu.SMEM((1,), F32),
         ),
         in_specs=[anywhere] * 10,
-        out_specs=(anywhere,) * 4,
+        out_specs=(anywhere,) * 3 + (pl.BlockSpec(memory_space=pltpu.SMEM),),
         scratch_shapes=[
             vmem(*focus.shape), pltpu.SMEM(permittivity.shape, F32), pltpu.SMEM(pml_x.shape, jnp.int32),
             pltpu.SMEM(pml_y.shape, jnp.int32), pltpu.SMEM(pml_z.shape, jnp.int32),
             pltpu.SMEM(monitor_z.shape, jnp.int32), pltpu.SMEM(omega.shape, F32),
-            vmem(1, 2 * WAVES * MON * 3, CX * CY), pltpu.SMEM((1,), F32),
+            vmem(1, 2 * WAVES * MON * 3, CX * CY),
             vmem(3, CX + 1, CY + 8, CZ), vmem(3, CX + 1, CY + 8, CZ), pltpu.VMEM((CX, CY, CZ), jnp.int32),
             vmem(CX, CY, CZ), vmem(CX, CY, CZ), vmem(CX, CY, CZ), vmem(CX, CY, CZ),
             vmem(CX, 128), vmem(CY, 128),
@@ -573,7 +559,7 @@
             vmem(early, 2, CY, 128), vmem(early, 2, CX, 128), vmem(early, 8, 128), vmem(early, 8, 128), vmem(3, CX, 128),
             vmem(early, 2, CY, 128), vmem(early, 2, CX, 128), vmem(early, 8, 128),
             vmem(6, early, 8, 128),
-            dma(13), dma(9), dma(STEPS + 1, 12), dma(STEPS + 1, 12),
+            dma(13), dma(8), dma(STEPS + 1, 12), dma(STEPS + 1, 12),
             dma(SLABS), dma(SLABS), dma(2), dma(2),
         ],
         compiler_params=pltpu.CompilerParams(
@@ -585,7 +571,8 @@
         out_shape=tuple(jax.ShapeDtypeStruct(a.shape, F32) for a in results),
         in_specs=[anywhere] * 4,
         out_specs=(anywhere,) * 4,
-        scratch_shapes=[vmem(3, CX, CY, CZ), vmem(3, CX, CY, CZ), vmem(*spectra.shape), pltpu.SMEM((1,), F32), dma(2, 8)],
+        scratch_shapes=[dma(8)],
+        compiler_params=pltpu.CompilerParams(vmem_limit_bytes=1024 * 1024),
     )(*results)
     return e_out, h_out, spectra, objective.reshape(())
 

time: 44.4 us -> 42.8 us (0.964)
  Pallas kernels: 43.7 us -> 42.1 us
    pallas_call x1, Pallas kernels: 2.28 us -> 1.26 us  [step(): pl.pallas_call(hand_on, out_shape=tuple((jax.ShapeDtypeStruct(a.shape, F3...]
    pallas_call x1, Pallas kernels: 41.4 us -> 40.8 us  [step(): pl.pallas_call(kernel, out_shape=(pltpu.VMEM(e_field.shape, F32), pltpu.V...]
where the time goes in v5:
time: 42.8 us; the launch traced here: 42.7 us
  Pallas kernels  42.1 us (98%)
  between operations  0.64 us (1%)
    pallas_call x1, Pallas kernels, step(): pl.pallas_call(kernel, out_shape=(pltpu.VMEM(e_field.shape, F32), pltpu.V...  40.8 us
    pallas_call x1, Pallas kernels, step(): pl.pallas_call(hand_on, out_shape=tuple((jax.ShapeDtypeStruct(a.shape, F3...  1.26 us

profile of v5, /device:TPU:1, one launch (start us, length us, event | category | flops | bytes accessed | tf_op | source)
XLA Modules:
  0.0 42.7 jit_solution(1489650964943540374)
XLA Ops:
  0.6 40.8 %shard_map.129 = (f32[1,3,16,32,128]{4,3,2,1,0:T(8,128)S(1)}, f32[1,3,16,32,128]{4,3,2,1,0:T(8,128)S(1)}, f32[1,72,512]{2,1,0:T(8,128)S(1)}, f32[1]{0:T(128)S(4)}) custom-call(f32[1,3,16,32,128]{4,3,2,1,0:T(8,128)} %e_in.1, f32[1,3,16,32,128]{4,3,2,1,0:T(8,128)} %h_in.1, s32[1,16,32,128]{3,2,1,0:T(8,128)} %m_in.1, f32[1,512]{1,0:T(1,128)} %focus_in.1, ...), custom_call_target="tpu_custom_call" | custom-call | tf_op jit(solution)/shard_map/pallas_call | solution.py:535
  41.5 1.3 %shard_map.130 = (f32[1,3,16,32,128]{4,3,2,1,0:T(8,128)}, f32[1,3,16,32,128]{4,3,2,1,0:T(8,128)}, f32[1,72,512]{2,1,0:T(8,128)}, f32[1]{0:T(128)}) custom-call(f32[1,3,16,32,128]{4,3,2,1,0:T(8,128)S(1)} %get-tuple-element.12.e_in, f32[1,3,16,32,128]{4,3,2,1,0:T(8,128)S(1)} %get-tuple-element.13.h_in, f32[1,72,512]{2,1,0:T(8,128)S(1)} %get-tuple-element.14.s_in, ...), custom_call_target="tpu_custom_call" | custom-call | tf_op jit(solution)/shard_map/pallas_call | solution.py:569

commit v6 on v5

--- a/solution.py
+++ b/solution.py
@@ -50,7 +50,7 @@
     s_hy, s_hz, r_hx, r_hy, r_hz,
     s_ey, s_ez, r_ex, r_ey, r_ez,
     s_ux, s_uy, s_uz, s_far, top, r_ux, r_uy, r_uz, r_edge,
-    local_sem, small_sem, send_sem, recv_sem, plane_send, plane_recv, total_send, total_recv,
+    local_sem, small_sem, send_sem, recv_sem, plane_send, plane_recv, total_send, total_recv, ready,
 ):
     tile = lax.axis_index("xy")
     slab = lax.axis_index("gz")
@@ -102,9 +102,8 @@
         k = (row * 2 + half + i) % (2 * TILES_X)
         return k // 2 * TILES_Y + col, k % 2 * 2 + core
 
-    for i in range(1, 2 * TILES_Y):
+    for i in (1, 2, 14, 15):
         greet(in_row(i))
-    for i in range(1, 2 * TILES_X):
         greet(in_column(i))
     greet((tile, SLABS - 1 - slab))
     for off in EDGES:
@@ -171,7 +170,7 @@
         total = pack(total, hs[1, x + 1, 8:8 + CY, :], 127, 64 + 4 * x)
     s_hz[...] = total
 
-    greeted = 2 * TILES_Y - 1 + 2 * TILES_X - 1 + 1
+    greeted = 9
     for off in EDGES:
         greeted = greeted + jnp.where(valid(off), 1, 0)
     pl.semaphore_wait(barrier, greeted)
@@ -183,6 +182,17 @@
     ]
     for move in opening:
         move.start()
+
+    def tell(k, distance):
+        for i in (distance, 16 - distance):
+            pl.semaphore_signal(ready.at[k, 0], inc=1, device_id=in_row(i), device_id_type=MESH)
+            pl.semaphore_signal(ready.at[k, 1], inc=1, device_id=in_column(i), device_id_type=MESH)
+
+    def hear(k):
+        pl.semaphore_wait(ready.at[k, 0], 2)
+        pl.semaphore_wait(ready.at[k, 1], 2)
+
+    tell(0, 2)
 
     for load in small:
         load.wait()
@@ -250,6 +260,8 @@
 
     for k in range(3):
         loads[4 + k].wait()
+    hear(0)
+    tell(1, 4)
     for move in opening:
         move.wait_recv()
     hs[1, 0, 8:8 + CY, :] = r_hx[0]
@@ -429,6 +441,8 @@
         moves = sum(electric_phase(n, False), [])
         extract_planes(n)
         magnetic_phase()
+        if n == 0:
+            hear(1)
         arrivals(n, moves)
         below_phase(n)
 
@@ -560,7 +574,7 @@
             vmem(early, 2, CY, 128), vmem(early, 2, CX, 128), vmem(early, 8, 128),
             vmem(6, early, 8, 128),
             dma(13), dma(8), dma(STEPS + 1, 12), dma(STEPS + 1, 12),
-            dma(SLABS), dma(SLABS), dma(2), dma(2),
+            dma(SLABS), dma(SLABS), dma(2), dma(2), pltpu.SemaphoreType.REGULAR((2, 2)),
         ],
         compiler_params=pltpu.CompilerParams(
             collective_id=0, has_side_effects=True, vmem_limit_bytes=60 * 1024 * 1024),

time: 42.8 us -> 42.2 us (0.986)
  Pallas kernels: 42.1 us -> 41.4 us
    pallas_call x1, Pallas kernels: 40.8 us -> 40.2 us  [step(): pl.pallas_call(kernel, out_shape=(pltpu.VMEM(e_field.shape, F32), pltpu.V...]
where the time goes in v6:
time: 42.2 us; the launch traced here: 42.1 us
  Pallas kernels  41.4 us (98%)
  between operations  0.64 us (2%)
    pallas_call x1, Pallas kernels, step(): pl.pallas_call(kernel, out_shape=(pltpu.VMEM(e_field.shape, F32), pltpu.V...  40.2 us
    pallas_call x1, Pallas kernels, step(): pl.pallas_call(hand_on, out_shape=tuple((jax.ShapeDtypeStruct(a.shape, F3...  1.26 us

profile of v6, /device:TPU:1, one launch (start us, length us, event | category | flops | bytes accessed | tf_op | source)
XLA Modules:
  0.0 42.1 jit_solution(12661841803085395520)
XLA Ops:
  0.6 40.2 %shard_map.129 = (f32[1,3,16,32,128]{4,3,2,1,0:T(8,128)S(1)}, f32[1,3,16,32,128]{4,3,2,1,0:T(8,128)S(1)}, f32[1,72,512]{2,1,0:T(8,128)S(1)}, f32[1]{0:T(128)S(4)}) custom-call(f32[1,3,16,32,128]{4,3,2,1,0:T(8,128)} %e_in.1, f32[1,3,16,32,128]{4,3,2,1,0:T(8,128)} %h_in.1, s32[1,16,32,128]{3,2,1,0:T(8,128)} %m_in.1, f32[1,512]{1,0:T(1,128)} %focus_in.1, ...), custom_call_target="tpu_custom_call" | custom-call | tf_op jit(solution)/shard_map/pallas_call | solution.py:549
  40.8 1.3 %shard_map.130 = (f32[1,3,16,32,128]{4,3,2,1,0:T(8,128)}, f32[1,3,16,32,128]{4,3,2,1,0:T(8,128)}, f32[1,72,512]{2,1,0:T(8,128)}, f32[1]{0:T(128)}) custom-call(f32[1,3,16,32,128]{4,3,2,1,0:T(8,128)S(1)} %get-tuple-element.12.e_in, f32[1,3,16,32,128]{4,3,2,1,0:T(8,128)S(1)} %get-tuple-element.13.h_in, f32[1,72,512]{2,1,0:T(8,128)S(1)} %get-tuple-element.14.s_in, ...), custom_call_target="tpu_custom_call" | custom-call | tf_op jit(solution)/shard_map/pallas_call | solution.py:583

commit v7 on v6

--- a/solution.py
+++ b/solution.py
@@ -49,7 +49,7 @@
     hy, hz, dax, day, daz, dby, dbz,
     s_hy, s_hz, r_hx, r_hy, r_hz,
     s_ey, s_ez, r_ex, r_ey, r_ez,
-    s_ux, s_uy, s_uz, s_far, top, r_ux, r_uy, r_uz, r_edge,
+    s_ux, s_uy, s_uz, s_far, s_first, top, r_ux, r_uy, r_uz, r_edge,
     local_sem, small_sem, send_sem, recv_sem, plane_send, plane_recv, total_send, total_recv, ready,
 ):
     tile = lax.axis_index("xy")
@@ -301,7 +301,7 @@
                 for k, e in enumerate((e0, e1, e2)):
                     top[k, x:x + 1, :] = e[CY - 1:CY]
                 high = pack(pack(high, e0, 127, 4 * x), e1, 127, 64 + 4 * x)
-                high2 = pack(pack(high2, e2, 127, 4 * x), e2, 127, 64 + 4 * x)
+                high2 = pack(high2, e2, 127, 4 * x)
                 if x == CX - 1:
                     e0z = jnp.where(lane32 == 127, 0.0, roll(e0, -1, 1))
                     e0y = jnp.where(row32 == CY - 1, 0.0, roll(e0, -1, 0))
@@ -316,22 +316,27 @@
             Move(n, 2, (0, 0, -1), s_ez.at[n], r_ez.at[n]),
         ]
         if not last:
-            sources = (s_ez.at[n], s_far.at[n], es.at[0, CX - 1, pl.ds(0, 8), :],
+            sources = (s_first.at[n, 0], s_first.at[n, 1], es.at[0, CX - 1, pl.ds(0, 8), :],
                        es.at[1, 0, pl.ds(CY - 8, 8), :], s_ez.at[n], s_far.at[n])
             edges = [Move(n, 6 + k, off, sources[k], r_edge.at[k, n]) for k, off in enumerate(EDGES)]
-            first_moves = edges[2:4] + [Move(n, 3, (1, 0, 0), s_ux.at[n], r_ux.at[n])] + first_moves
-            moves = [moves[0], Move(n, 4, (0, 1, 0), s_uy.at[n], r_uy.at[n])] + edges[0:2] + edges[4:6] + [
+            first_moves = edges[2:4] + [Move(n, 3, (1, 0, 0), s_ux.at[n], r_ux.at[n])] + first_moves + edges[0:2]
+            moves = [moves[0], Move(n, 4, (0, 1, 0), s_uy.at[n], r_uy.at[n])] + edges[4:6] + [
                 moves[1], Move(n, 5, (0, 0, 1), s_uz.at[n], r_uz.at[n])]
-        packs = electric_planes(n, (0,) if last else (0, CX - 1), last, (zero8, zero8, zero8))
-        for move in first_moves:
-            move.start()
-        low, high, high2 = electric_planes(n, range(1, CX if last else CX - 1), last, packs)
+        packs = (zero8, zero8, zero8) if last else electric_planes(n, (0, CX - 1), last, (zero8, zero8, zero8))
+        if not last:
+            s_first[n, 0] = packs[0]
+            s_first[n, 1] = packs[2]
+        if not last:
+            for move in first_moves:
+                move.start()
+        low, high, high2 = electric_planes(n, range(CX) if last else range(1, CX - 1), last, packs)
         s_ez[n] = low
         if not last:
             e0, e1, e2 = top[0], top[1], top[2]
             s_uy[n, 0] = (e1 - jnp.where(lane16 == 127, 0.0, roll(e1, -1, 1))) - e2
             s_uy[n, 1] = (jnp.where(row16 == CX - 1, 0.0, roll(e1, -1, 0)) - e1) + e0
             s_far[n] = high2
+            high2 = high2 + roll(high2, 64, 1)
             up = roll(high2, -1, 0)
             e2y = jnp.where(row8 < 7, up, jnp.where(lane8 % 4 == 3, 0.0, roll(up, -1, 1)))
             e2x = jnp.where(lane8 >= 124, 0.0, roll(high2, -4, 1))
@@ -476,7 +481,7 @@
 
     first[pl.ds(col * 2 + core, 1), :] = part
     send_totals(0, col * 2 + core, in_row)
-    for move in later:
+    for move in moves + later:
         move.start()
     for i in range(1, SLABS):
         plane_move(i, slab).start()
@@ -570,7 +575,8 @@
             vmem(2, CX, 128), vmem(8, 128), vmem(2, CY, 128), vmem(2, CX, 128), vmem(8, 128),
             vmem(STEPS, 2, CX, 128), vmem(STEPS, 8, 128),
             vmem(STEPS, 2, CY, 128), vmem(STEPS, 2, CX, 128), vmem(STEPS, 8, 128),
-            vmem(early, 2, CY, 128), vmem(early, 2, CX, 128), vmem(early, 8, 128), vmem(early, 8, 128), vmem(3, CX, 128),
+            vmem(early, 2, CY, 128), vmem(early, 2, CX, 128), vmem(early, 8, 128), vmem(early, 8, 128),
+            vmem(early, 2, 8, 128), vmem(3, CX, 128),
             vmem(early, 2, CY, 128), vmem(early, 2, CX, 128), vmem(early, 8, 128),
             vmem(6, early, 8, 128),
             dma(13), dma(8), dma(STEPS + 1, 12), dma(STEPS + 1, 12),

time: 42.2 us -> 42 us (level)
  no operation moved by 1% of the time
where the time goes in v7:
time: 42 us; the launch traced here: 41.9 us
  Pallas kernels  41.3 us (98%)
  between operations  0.64 us (2%)
    pallas_call x1, Pallas kernels, step(): pl.pallas_call(kernel, out_shape=(pltpu.VMEM(e_field.shape, F32), pltpu.V...  40 us
    pallas_call x1, Pallas kernels, step(): pl.pallas_call(hand_on, out_shape=tuple((jax.ShapeDtypeStruct(a.shape, F3...  1.26 us

profile of v7, /device:TPU:1, one launch (start us, length us, event | category | flops | bytes accessed | tf_op | source)
XLA Modules:
  0.0 41.9 jit_solution(14276558978519701480)
XLA Ops:
  0.6 40.0 %shard_map.129 = (f32[1,3,16,32,128]{4,3,2,1,0:T(8,128)S(1)}, f32[1,3,16,32,128]{4,3,2,1,0:T(8,128)S(1)}, f32[1,72,512]{2,1,0:T(8,128)S(1)}, f32[1]{0:T(128)S(4)}) custom-call(f32[1,3,16,32,128]{4,3,2,1,0:T(8,128)} %e_in.1, f32[1,3,16,32,128]{4,3,2,1,0:T(8,128)} %h_in.1, s32[1,16,32,128]{3,2,1,0:T(8,128)} %m_in.1, f32[1,512]{1,0:T(1,128)} %focus_in.1, ...), custom_call_target="tpu_custom_call" | custom-call | tf_op jit(solution)/shard_map/pallas_call | solution.py:554
  40.7 1.3 %shard_map.130 = (f32[1,3,16,32,128]{4,3,2,1,0:T(8,128)}, f32[1,3,16,32,128]{4,3,2,1,0:T(8,128)}, f32[1,72,512]{2,1,0:T(8,128)}, f32[1]{0:T(128)}) custom-call(f32[1,3,16,32,128]{4,3,2,1,0:T(8,128)S(1)} %get-tuple-element.12.e_in, f32[1,3,16,32,128]{4,3,2,1,0:T(8,128)S(1)} %get-tuple-element.13.h_in, f32[1,72,512]{2,1,0:T(8,128)S(1)} %get-tuple-element.14.s_in, ...), custom_call_target="tpu_custom_call" | custom-call | tf_op jit(solution)/shard_map/pallas_call | solution.py:589
